TPU v7x, 512 devices: a whole 4x8x8 slice. The times are simulated.
512 devices in a mesh: leaf: 64 (over y, x, core), head: 8 (over z).
Axes of the slice: x: 4, y: 8, z: 8, core: 2. Of those that a mesh axis runs over, the one named last changes fastest.
Arguments:
- queries: bfloat16 [16384, 6144], P('leaf', 'head'), may hold values from -6 to 6
- key_rows: bfloat16 [16384, 1024], P(('leaf', 'head')), may hold values from -6 to 6
- value_rows: bfloat16 [16384, 1024], P(('leaf', 'head')), may hold values from -6 to 6
- out_grad: bfloat16 [16384, 6144], P('leaf', 'head'), may hold values from -6 to 6
- ancestry: int32 [128, 128], replicated, may hold values from 0 to 1, as said below
- block_fill: int32 [128], replicated, may hold values from 32 to 128, as said below
Outputs:
- attn_out: bfloat16 [16384, 6144], P('leaf', 'head')
- query_grad: bfloat16 [16384, 6144], P('leaf', 'head')
- key_grad: bfloat16 [16384, 1024], P('leaf', 'head')
- value_grad: bfloat16 [16384, 1024], P('leaf', 'head')
Inputs may be any that keep to these rules, and one draw needn't show every extreme that they name: ancestry[b, a] is 1 exactly when a = b, a = 0, or block a is an ancestor of block b in the tree of reasoning steps, else 0. Every ancestor a > 0 of b has a < b and a >= (b // 2 - 3) * 2; some block has an ancestor at exactly that limit. block_fill[b] is 128 when block b + 1 continues the step of block b.
All inputs are finite; a program needn't handle non-finite values.
Results may differ from a plain program's by a relative error of at most 0.012.
The roundings to bfloat16 on the way count: a program that leaves them out, or rounds other values in their place, can miss the bound.
Values may be sent and summed in bfloat16 or wider, within the bound.
A program may use at most 64 MiB of HBM per device.

v0:
```python
import math

import jax
import jax.numpy as jnp
from jax import lax
from jax.sharding import PartitionSpec as P

HD = 128
BLK = 128
REACH = 4


neg_fill = -1e30


def broadcast(value, axis, source):
    kept = jnp.where(lax.axis_index(axis) == source, value, 0).astype(value.dtype)
    return lax.psum(kept, axis)


def shifted(array, axis, by):
    peers = lax.axis_size(axis)
    pairs = [(i, i + by) for i in range(peers) if 0 <= i + by < peers]
    return lax.ppermute(array, axis, pairs)


def on_device(queries, key_rows, value_rows, out_grad, ancestry, block_fill):
    leaf_index = lax.axis_index("leaf")
    stacked = jnp.stack([key_rows, value_rows])
    kv_local = lax.all_to_all(stacked, "head", split_axis=2, concat_axis=1, tiled=True)
    tok_rows = queries.shape[0]
    width_kv = kv_local.shape[2]
    heads_here = queries.shape[1] // HD
    blocks_dev = tok_rows // BLK
    inv_scale = 1.0 / math.sqrt(HD)
    kv_prompt = broadcast(kv_local[:, :BLK], "leaf", 0)
    pieces = [kv_local]
    for offset in range(1, REACH):
        pieces.append(shifted(kv_local, "leaf", offset))
    window = jnp.concatenate(
        [kv_prompt] + [pieces[offset] for offset in range(REACH - 1, -1, -1)], axis=1
    )
    key_all = window[0]
    value_all = window[1]
    wide = window.shape[1]
    anc_rows = lax.dynamic_slice_in_dim(ancestry, leaf_index * blocks_dev, blocks_dev, 0)
    anc_pad = jnp.pad(anc_rows, ((0, 0), ((REACH - 1) * blocks_dev, 0)))
    anc_window = lax.dynamic_slice_in_dim(anc_pad, leaf_index * blocks_dev, REACH * blocks_dev, 1)
    col_global = (leaf_index - (REACH - 1)) * blocks_dev + jnp.arange(
        REACH * blocks_dev, dtype=jnp.int32
    )
    anc_window = jnp.where(col_global[None, :] >= 1, anc_window, 0)
    block_links = jnp.concatenate([anc_rows[:, :1], anc_window], axis=1)
    fill_pad = jnp.pad(block_fill, (((REACH - 1) * blocks_dev, 0),))
    fill_window = lax.dynamic_slice_in_dim(fill_pad, leaf_index * blocks_dev, REACH * blocks_dev, 0)
    fills = jnp.concatenate([block_fill[:1], fill_window])
    key_pos = jnp.arange(wide, dtype=jnp.int32)
    key_valid = key_pos % BLK < jnp.repeat(fills, BLK)
    key_global = jnp.concatenate(
        [
            jnp.arange(BLK, dtype=jnp.int32),
            (leaf_index - (REACH - 1)) * tok_rows + jnp.arange(REACH * tok_rows, dtype=jnp.int32),
        ]
    )
    query_global = leaf_index * tok_rows + jnp.arange(tok_rows, dtype=jnp.int32)
    linked = jnp.repeat(jnp.repeat(block_links, BLK, axis=0), BLK, axis=1) == 1
    allowed = linked & key_valid[None, :] & (key_global[None, :] <= query_global[:, None])

    def attend_head(head_idx, running):
        out_acc, dq_acc, grad_acc = running
        q_head = lax.dynamic_slice_in_dim(queries, head_idx * HD, HD, 1)
        g_head = lax.dynamic_slice_in_dim(out_grad, head_idx * HD, HD, 1)
        scores = (
            lax.dot_general(
                q_head, key_all, (((1,), (1,)), ((), ())), preferred_element_type=jnp.float32
            )
            * inv_scale
        )
        scores = jnp.where(allowed, scores, neg_fill)
        row_max = jnp.max(scores, axis=1, keepdims=True)
        log_total = row_max + jnp.log(jnp.sum(jnp.exp(scores - row_max), axis=1, keepdims=True))
        weights = jnp.exp(scores - log_total)
        weights_b = weights.astype(jnp.bfloat16)
        head_out = jnp.dot(weights_b, value_all, preferred_element_type=jnp.float32)
        d_weights = lax.dot_general(
            g_head, value_all, (((1,), (1,)), ((), ())), preferred_element_type=jnp.float32
        )
        row_delta = jnp.sum(g_head.astype(jnp.float32) * head_out, axis=1, keepdims=True)
        d_scores = (weights * (d_weights - row_delta)).astype(jnp.bfloat16)
        dq_head = jnp.dot(d_scores, key_all, preferred_element_type=jnp.float32) * inv_scale
        dk_head = (
            lax.dot_general(
                d_scores, q_head, (((0,), (0,)), ((), ())), preferred_element_type=jnp.float32
            )
            * inv_scale
        )
        dv_head = lax.dot_general(
            weights_b, g_head, (((0,), (0,)), ((), ())), preferred_element_type=jnp.float32
        )
        out_acc = lax.dynamic_update_slice_in_dim(
            out_acc, head_out.astype(jnp.bfloat16), head_idx * HD, 1
        )
        dq_acc = lax.dynamic_update_slice_in_dim(
            dq_acc, dq_head.astype(jnp.bfloat16), head_idx * HD, 1
        )
        previous = grad_acc
        grad_acc = previous + jnp.stack([dk_head, dv_head])
        return (out_acc, dq_acc, grad_acc)

    starting = (
        jnp.zeros(queries.shape, jnp.bfloat16),
        jnp.zeros(queries.shape, jnp.bfloat16),
        jnp.zeros((2, wide, width_kv), jnp.float32),
    )
    attn_out, query_grad, grad_acc = lax.fori_loop(0, heads_here, attend_head, starting)

    def window_part(offset):
        first_row = BLK + (REACH - 1 - offset) * tok_rows
        return grad_acc[:, first_row : first_row + tok_rows]

    grad_total = window_part(0)
    for offset in range(1, REACH):
        grad_total = grad_total + shifted(window_part(offset), "leaf", -offset)
    prompt_sum = lax.psum(grad_acc[:, :BLK], "leaf")
    is_root = leaf_index == 0
    head_rows = grad_total[:, :BLK] + jnp.where(is_root, prompt_sum, 0.0)
    grad_total = jnp.concatenate([head_rows, grad_total[:, BLK:]], axis=1)
    return (
        attn_out,
        query_grad,
        grad_total[0].astype(jnp.bfloat16),
        grad_total[1].astype(jnp.bfloat16),
    )


def solution(mesh):
    placed = (
        P("leaf", "head"),
        P(("leaf", "head"), None),
        P(("leaf", "head"), None),
        P("leaf", "head"),
        P(),
        P(),
    )
    return jax.shard_map(
        on_device,
        mesh=mesh,
        in_specs=placed,
        out_specs=(P("leaf", "head"), P("leaf", "head"), P("leaf", "head"), P("leaf", "head")),
        check_vma=False,
    )
```

profile of v0, /device:TPU:1, one launch (start us, length us, event | category | flops | bytes accessed | tf_op | source)
XLA Modules:
  0.0 459.7 jit_solution(6728857524317168868)
XLA Ops:
  9.7 10.9 %all-to-all-start = ((bf16[8,2,4096]{2,1,0:T(2,128)(2,1)}), bf16[8,2,4096]{2,1,0:T(2,128)(2,1)S(1)}, u32[]{:S(2)}, u32[]{:S(2)}) async-start(bf16[8,2,4096]{2,1,0:T(2,128)(2,1)} %reshape.59), calls=%async_computation | async-start | bytes 262144 | tf_op jit(solution)/shard_map/all_to_all | solution.py:30
  21.3 7.0 %all-to-all-done = bf16[8,2,4096]{2,1,0:T(2,128)(2,1)S(1)} async-done(((bf16[8,2,4096]{2,1,0:T(2,128)(2,1)}), bf16[8,2,4096]{2,1,0:T(2,128)(2,1)S(1)}, u32[]{:S(2)}, u32[]{:S(2)}) %all-to-all-start) | async-done | bytes 131104 | tf_op jit(solution)/shard_map/all_to_all | solution.py:30
  29.0 6.8 %collective-permute-start = (bf16[2,256,128]{2,1,0:T(8,128)(2,1)S(1)}, bf16[2,256,128]{2,1,0:T(8,128)(2,1)S(1)}, u32[]{:S(2)}, u32[]{:S(2)}) collective-permute-start(bf16[2,256,128]{2,1,0:T(8,128)(2,1)S(1)} %bitcast.64), channel_id=1, source_target_pairs={{0,24},{8,32},{16,40},{24,48},{32,56},{40,64},{48,72},{56,80},{64,... | collective-permute-start | bytes 393224 | tf_op jit(solution)/shard_map/ppermute | solution.py:24
  36.6 1.9 collective-permute-start.2
  38.5 2.2 collective-permute-start.1
  40.7 169.0 %all-reduce.5.cloned.1.call-done = bf16[2,128,128]{2,1,0:T(8,128)(2,1)} async-done(((bf16[2,128,128]{2,1,0:T(8,128)(2,1)}), bf16[2,128,128]{2,1,0:T(8,128)(2,1)}) %all-reduce.5.cloned.1.call-update) | async-done | bytes 65552 | tf_op jit(solution)/shard_map/psum | solution.py:18
  212.3 46.6 %while.18 = (s32[]{:T(128)}, bf16[256,768]{1,0:T(8,128)(2,1)}, bf16[256,768]{1,0:T(8,128)(2,1)}, f32[2,1152,128]{2,1,0:T(8,128)S(1)}, bf16[256,768]{1,0:T(8,128)...) while((s32[]{:T(128)}, bf16[256,768]{1,0:T(8,128)(2,1)}, ...), condition=%wide.region_5.6_spmd.clone, body=%wide.region_1.5_spmd.clone.sunk | while | flops 458931712 | bytes 15749225 | solution.py:115
  213.8 1.4 fusion.55
  218.5 1.2 fusion.58
  221.6 1.4 fusion.55
  226.3 1.2 fusion.58
  229.3 1.4 fusion.55
  234.1 1.2 fusion.58
  237.1 1.4 fusion.55
  241.9 1.2 fusion.58
  244.9 1.4 fusion.55
  249.6 1.2 fusion.58
  252.7 1.4 fusion.55
  259.0 2.3 collective-permute-start.3
  261.3 1.3 collective-permute-start.4
  262.6 1.3 collective-permute-start.5
  264.6 3.1 collective-permute-done.3
  267.7 5.5 %collective-permute-done.4 = f32[2,256,128]{2,1,0:T(8,128)S(1)} collective-permute-done((f32[2,256,128]{2,1,0:T(8,128)S(1)}, f32[2,256,128]{2,1,0:T(8,128)S(1)}, u32[]{:S(2)}, u32[]{:S(2)}) %collective-permute-start.4) | collective-permute-done | bytes 262176 | tf_op jit(solution)/shard_map/ppermute | solution.py:24
  273.3 178.8 %all-reduce.7.cloned.1.call-done = f32[2,128,128]{2,1,0:T(8,128)} async-done(((f32[2,128,128]{2,1,0:T(8,128)}), f32[2,128,128]{2,1,0:T(8,128)}) %all-reduce.7.cloned.1.call-update) | async-done | bytes 131088 | tf_op jit(solution)/shard_map/psum | solution.py:124
  (127 shorter events, 40.1 us)
Async XLA Ops:
  7.2 13.7 %copy-start = (s32[128,128]{1,0:T(8,128)S(1)}, s32[128,128]{1,0:T(8,128)}, u32[]{:S(2)}) copy-start(s32[128,128]{1,0:T(8,128)} %param.12) | copy-start | bytes 196612
  7.2 13.4 %copy-start.1 = (s32[128]{0:T(128)S(1)}, s32[128]{0:T(128)}, u32[]{:S(2)}) copy-start(s32[128]{0:T(128)} %param.13) | copy-start | bytes 1540
  9.7 18.6 %all-to-all-start = ((bf16[8,2,4096]{2,1,0:T(2,128)(2,1)}), bf16[8,2,4096]{2,1,0:T(2,128)(2,1)S(1)}, u32[]{:S(2)}, u32[]{:S(2)}) async-start(bf16[8,2,4096]{2,1,0:T(2,128)(2,1)} %reshape.59), calls=%async_computation | async-start | bytes 262144 | tf_op jit(solution)/shard_map/all_to_all | solution.py:30
  20.5 189.2 %all-reduce.5.cloned.1.call-start = ((), (), s32[]{:S(2)}) async-start(), calls=%async_computation.1 | async-start | bytes 131072 | tf_op jit(solution)/shard_map/psum | solution.py:18
  29.0 181.7 %collective-permute-start = (bf16[2,256,128]{2,1,0:T(8,128)(2,1)S(1)}, bf16[2,256,128]{2,1,0:T(8,128)(2,1)S(1)}, u32[]{:S(2)}, u32[]{:S(2)}) collective-permute-start(bf16[2,256,128]{2,1,0:T(8,128)(2,1)S(1)} %bitcast.64), channel_id=1, source_target_pairs={{0,24},{8,32},{16,40},{24,48},{32,56},{40,64},{48,72},{56,80},{64,... | collective-permute-start | bytes 393224 | tf_op jit(solution)/shard_map/ppermute | solution.py:24
  36.5 415.7 %all-reduce.7.cloned.1.call-start = ((), (), s32[]{:S(2)}) async-start(), calls=%async_computation.2 | async-start | bytes 262144 | tf_op jit(solution)/shard_map/psum | solution.py:124
  36.6 174.1 %collective-permute-start.2 = (bf16[2,256,128]{2,1,0:T(8,128)(2,1)S(1)}, bf16[2,256,128]{2,1,0:T(8,128)(2,1)S(1)}, u32[]{:S(2)}, u32[]{:S(2)}) collective-permute-start(bf16[2,256,128]{2,1,0:T(8,128)(2,1)S(1)} %bitcast.66), channel_id=1, source_target_pairs={{0,8},{8,16},{16,24},{24,32},{32,40},{40,48},{48,56},{56,64},{64,7... | collective-permute-start | bytes 393224 | tf_op jit(solution)/shard_map/ppermute | solution.py:24
  38.5 172.1 %collective-permute-start.1 = (bf16[2,256,128]{2,1,0:T(8,128)(2,1)S(1)}, bf16[2,256,128]{2,1,0:T(8,128)(2,1)S(1)}, u32[]{:S(2)}, u32[]{:S(2)}) collective-permute-start(bf16[2,256,128]{2,1,0:T(8,128)(2,1)S(1)} %bitcast.67), channel_id=1, source_target_pairs={{0,16},{8,24},{16,32},{24,40},{32,48},{40,56},{48,64},{56,72},{64,... | collective-permute-start | bytes 393224 | tf_op jit(solution)/shard_map/ppermute | solution.py:24
  259.0 8.7 %collective-permute-start.3 = (f32[2,256,128]{2,1,0:T(8,128)S(1)}, f32[2,256,128]{2,1,0:T(8,128)S(1)}, u32[]{:S(2)}, u32[]{:S(2)}) collective-permute-start(f32[2,256,128]{2,1,0:T(8,128)S(1)} %get-tuple-element.317), channel_id=1, source_target_pairs={{8,0},{16,8},{24,16},{32,24},{40,32},{48,40},{56,48},{64,56},{72,6... | collective-permute-start | bytes 786440 | tf_op jit(solution)/shard_map/ppermute | solution.py:24
  261.3 11.9 %collective-permute-start.4 = (f32[2,256,128]{2,1,0:T(8,128)S(1)}, f32[2,256,128]{2,1,0:T(8,128)S(1)}, u32[]{:S(2)}, u32[]{:S(2)}) collective-permute-start(f32[2,256,128]{2,1,0:T(8,128)S(1)} %get-tuple-element.318), channel_id=1, source_target_pairs={{16,0},{24,8},{32,16},{40,24},{48,32},{56,40},{64,48},{72,56},{80,... | collective-permute-start | bytes 786440 | tf_op jit(solution)/shard_map/ppermute | solution.py:24
  262.6 10.6 %collective-permute-start.5 = (f32[2,256,128]{2,1,0:T(8,128)S(1)}, f32[2,256,128]{2,1,0:T(8,128)S(1)}, u32[]{:S(2)}, u32[]{:S(2)}) collective-permute-start(f32[2,256,128]{2,1,0:T(8,128)S(1)} %get-tuple-element.319), channel_id=1, source_target_pairs={{24,0},{32,8},{40,16},{48,24},{56,32},{64,40},{72,48},{80,56},{88,... | collective-permute-start | bytes 786440 | tf_op jit(solution)/shard_map/ppermute | solution.py:24
Sparse Core Ops, SparseCore 0:
  36.6 173.1 all-reduce.4
  264.7 187.3 all-reduce.6
where the time goes:
time: 461 us; the launch traced here: 460 us
  waiting for transfers between devices  364 us (79%)
  matrix products  29 us (6%)
  starting transfers between devices  26.8 us (6%)
  local copies, waits for them, and re-layouts  19.5 us (4%)
  between operations  14.3 us (3%)
  other arithmetic  6.07 us (1%)
    psum x1, waiting for transfers between devices, on_device(): prompt_sum = lax.psum(grad_acc[:, :BLK], 'leaf')  179 us
    psum x1, waiting for transfers between devices, broadcast(): return lax.psum(kept, axis)  169 us
    ppermute x6, starting transfers between devices, shifted(): return lax.ppermute(array, axis, pairs)  15.9 us
    all_to_all x1, starting transfers between devices, on_device(): lax.all_to_all(stacked, 'head', split_axis=2, concat_axis=1, tiled=True)  10.9 us
  transfers between devices with their start and end apart: 9, of which 5 were waited for; matrix products, arithmetic and copies ran while one was open for 1% of the time, Pallas kernels for 0%

commit v1 on v0

v1 whole, which is shorter than its diff:
```python
import functools
import math

import jax
import jax.numpy as jnp
from jax import lax
from jax.experimental import pallas as pl
from jax.experimental.pallas import tpu as pltpu
from jax.sharding import PartitionSpec as P

HD = 128
BLK = 128
REACH = 4
ROW = 8
MESH = pl.DeviceIdType.MESH
NEG = -1e30
NT = (((1,), (1,)), ((), ()))
NN = (((1,), (0,)), ((), ()))
dot = functools.partial(lax.dot_general, preferred_element_type=jnp.float32)


def kernel(
    leaves, groups, queries, key_rows, value_rows, out_grad, ancestry, block_fill,
    attn_out, query_grad, key_grad, value_grad,
    q, g, kv_in, win, win_t, bias, scores, d_weights, row_max, probs, attn, dq,
    grads, own_grad, prompt_grad, prompt_bf, near, part_y, sum_y, part_x, sum_x, prompt_sum,
    final, anc,
    load_sem, store_sem, a2a_send, a2a_recv, shift_send, shift_recv, root_send, root_recv,
    gather_send, gather_recv, grad_send, grad_recv, ry_send, ry_recv, rx_send, rx_recv, rr_send, rr_recv,
):
    leaf = lax.axis_index("leaf")
    head = lax.axis_index("head")
    tok = q.shape[0]
    heads_here = q.shape[1] // HD
    rows_in = kv_in.shape[1]
    rows_y = leaves // ROW
    piece = BLK // rows_y
    wide = win.shape[1]
    own0 = wide - tok
    y = leaf // ROW
    xc = leaf % ROW
    inv_scale = 1.0 / math.sqrt(HD)
    log_scale = inv_scale * math.log2(math.e)

    base = pl.multiple_of((2 * leaf) // 8 * 8, 8)
    loads = [
        pltpu.make_async_copy(key_rows, kv_in.at[0], load_sem.at[0]),
        pltpu.make_async_copy(value_rows, kv_in.at[1], load_sem.at[1]),
        pltpu.make_async_copy(queries, q, load_sem.at[2]),
        pltpu.make_async_copy(out_grad, g, load_sem.at[3]),
        pltpu.make_async_copy(ancestry.at[pl.ds(base, 8)], anc, load_sem.at[4]),
    ]
    for load in loads:
        load.start()

    barrier = pltpu.get_barrier_semaphore()

    def greet(leaf_to, head_to):
        pl.semaphore_signal(barrier, inc=1, device_id=(leaf_to, head_to), device_id_type=MESH)

    for off in range(1, groups):
        greet(leaf, lax.rem(head + off, groups))
    for off in range(1, rows_y):
        greet(lax.rem(y + off, rows_y) * ROW + xc, head)
    for off in range(1, REACH):
        pl.when(leaf >= off)(functools.partial(greet, leaf - off, head))
        pl.when(leaf + off < leaves)(functools.partial(greet, leaf + off, head))

    @pl.when(leaf > 0)
    def _():
        greet(0, head)

    @pl.when(xc == 0)
    def _():
        for off in range(1, ROW):
            greet(leaf + off, head)

    for load in loads[:2]:
        load.wait()
    greeted = groups - 1 + rows_y - 1 + jnp.minimum(leaf, REACH - 1) + jnp.minimum(leaves - 1 - leaf, REACH - 1)
    greeted += jnp.where(xc > 0, 1, 0) + jnp.where(leaf == 0, leaves - 1, 0)
    pl.semaphore_wait(barrier, greeted)

    def remote(src, dst, send, recv, leaf_to, head_to):
        return pltpu.make_async_remote_copy(
            src_ref=src, dst_ref=dst, send_sem=send, recv_sem=recv,
            device_id=(leaf_to, head_to), device_id_type=MESH,
        )

    def a2a_copy(off):
        to = lax.rem(head + off, groups)
        return remote(
            kv_in.at[:, :, pl.ds(pl.multiple_of(to * HD, HD), HD)],
            win.at[:, pl.ds(pl.multiple_of(own0 + head * rows_in, 32), rows_in), :],
            a2a_send.at[off], a2a_recv.at[off], leaf, to,
        )

    for off in range(1, groups):
        a2a_copy(off).start()
    win[:, pl.ds(pl.multiple_of(own0 + head * rows_in, 32), rows_in), :] = kv_in[
        :, :, pl.ds(pl.multiple_of(head * HD, HD), HD)
    ]
    for off in range(1, REACH):
        rows = pl.ds(own0 - off * tok, tok)

        @pl.when(leaf < off)
        def _():
            win[:, rows, :] = jnp.zeros((2, tok, HD), win.dtype)

    loads[4].wait()
    key_iota = lax.broadcasted_iota(jnp.int32, (BLK, BLK), 0)
    query_iota = lax.broadcasted_iota(jnp.int32, (BLK, BLK), 1)
    blocks_dev = tok // BLK
    for col in range(wide // BLK):
        block = 0 if col == 0 else (leaf - (REACH - 1)) * blocks_dev + col - 1
        at = 0 if col == 0 else jnp.maximum(block, 0)
        fill = block_fill[at]
        for row in range(blocks_dev):
            link = anc[2 * leaf - base + row, at]
            if col > 0:
                link = jnp.where(block >= 1, link, 0)
            limit = jnp.where(link == 1, fill, 0)
            allowed = (key_iota < limit) & (
                key_iota + block * BLK <= query_iota + (leaf * blocks_dev + row) * BLK
            )
            bias[col * BLK : (col + 1) * BLK, row * BLK : (row + 1) * BLK] = jnp.where(allowed, 0.0, NEG)
    row_max[...] = jnp.full_like(row_max, NEG)

    for off in range(1, groups):
        a2a_copy(off).wait_recv()

    def shift_copy(off):
        return remote(
            win.at[:, pl.ds(own0, tok), :], win.at[:, pl.ds(own0 - off * tok, tok), :],
            shift_send.at[off], shift_recv.at[off], leaf + off, head,
        )

    def root_copy(to):
        at = to // ROW * piece
        return remote(
            win.at[:, pl.ds(pl.multiple_of(own0 + at, piece), piece), :],
            win.at[:, pl.ds(pl.multiple_of(at, piece), piece), :],
            root_send.at[to], root_recv, to, head,
        )

    @pl.when(leaf == 0)
    def _():
        @pl.loop(1, leaves)
        def _(to):
            root_copy(to).start()

        win[:, :piece, :] = win[:, own0 : own0 + piece, :]

    for off in range(1, REACH):
        pl.when(leaf + off < leaves)(lambda off=off: shift_copy(off).start())

    loads[2].wait()
    loads[3].wait()

    def meet(first, count):
        rows = slice(first, first + count)
        keys, values, added = win[0, rows], win[1, rows], bias[rows]
        for j in range(heads_here):
            cols = slice(j * HD, (j + 1) * HD)
            part = dot(keys, q[:, cols], NT) + added
            scores[j, rows] = part
            row_max[j] = jnp.maximum(row_max[j], part.reshape(count // 8, 8, tok).max(0))
            d_weights[j, rows] = dot(values, g[:, cols], NT)

    meet(own0, tok)

    my_piece = pl.ds(pl.multiple_of(y * piece, piece), piece)

    def gather_copy(off):
        return remote(
            win.at[:, my_piece, :], win.at[:, my_piece, :],
            gather_send.at[off], gather_recv.at[off], lax.rem(y + off, rows_y) * ROW + xc, head,
        )

    @pl.when(leaf > 0)
    def _():
        root_copy(leaf).wait_recv()

    for off in range(1, rows_y):
        gather_copy(off).start()

    for off in range(1, REACH):
        pl.when(leaf >= off)(lambda off=off: shift_copy(off).wait_recv())
        meet(own0 - off * tok, tok)
    for off in range(1, rows_y):
        gather_copy(off).wait_recv()
    meet(0, BLK)
    win_t[0] = win[0].T
    win_t[1] = win[1].T

    step = BLK
    for j in range(heads_here):
        cols = slice(j * HD, (j + 1) * HD)
        top = jnp.max(row_max[j], axis=0, keepdims=True) * log_scale
        total = jnp.zeros((8, tok), jnp.float32)
        delta = jnp.zeros((8, tok), jnp.float32)
        for r in range(0, wide, step):
            rows = slice(r, r + step)
            e = jnp.exp2(scores[j, rows] * log_scale - top)
            scores[j, rows] = e
            total += e.reshape(step // 8, 8, tok).sum(0)
            delta += (e * d_weights[j, rows]).reshape(step // 8, 8, tok).sum(0)
        inverse = 1.0 / total.sum(0, keepdims=True)
        delta = delta.sum(0, keepdims=True) * inverse
        for r in range(0, wide, step):
            rows = slice(r, r + step)
            w = scores[j, rows] * inverse
            probs[0, j, rows] = w.astype(jnp.bfloat16)
            probs[1, j, rows] = (w * (d_weights[j, rows] - delta)).astype(jnp.bfloat16)
        attn[:, cols] = dot(win_t[1], probs[0, j], NN).T.astype(jnp.bfloat16)
    out_copy = pltpu.make_async_copy(attn, attn_out, store_sem.at[0])
    out_copy.start()

    def grad_of(first, count):
        dk = jnp.zeros((count, HD), jnp.float32)
        dv = jnp.zeros((count, HD), jnp.float32)
        for j in range(heads_here):
            cols = slice(j * HD, (j + 1) * HD)
            dk += dot(probs[1, j, first : first + count], q[:, cols], NN)
            dv += dot(probs[0, j, first : first + count], g[:, cols], NN)
        return dk * inv_scale, dv

    def ry_copy(off):
        to = lax.rem(y + off, rows_y)
        return remote(
            prompt_bf.at[:, pl.ds(pl.multiple_of(to * piece, piece), piece), :], part_y.at[off],
            ry_send.at[off], ry_recv.at[off], to * ROW + xc, head,
        )

    dk, dv = grad_of(0, BLK)
    prompt_grad[0], prompt_grad[1] = dk, dv
    prompt_bf[0], prompt_bf[1] = dk.astype(jnp.bfloat16), dv.astype(jnp.bfloat16)
    for off in range(1, rows_y):
        ry_copy(off).start()

    def grad_copy(off):
        return remote(
            grads.at[off], near.at[off], grad_send.at[off], grad_recv.at[off], leaf - off, head
        )

    for off in range(REACH - 1, 0, -1):
        dk, dv = grad_of(own0 - off * tok, tok)
        grads[off, 0], grads[off, 1] = dk.astype(jnp.bfloat16), dv.astype(jnp.bfloat16)
        pl.when(leaf >= off)(lambda off=off: grad_copy(off).start())

    for off in range(1, rows_y):
        ry_copy(off).wait_recv()
    sum_y[...] = prompt_grad[:, my_piece, :]
    for off in range(1, rows_y):
        sum_y[...] += part_y[off].astype(jnp.float32)

    def rx_copy(slot):
        return remote(sum_x.at[0], part_x.at[slot], rx_send, rx_recv.at[slot], y * ROW, head)

    sum_x[0] = sum_y[...].astype(jnp.bfloat16)

    @pl.when(xc > 0)
    def _():
        rx_copy(xc).start()

    own_grad[0], own_grad[1] = grad_of(own0, tok)

    def rr_copy():
        return remote(sum_x.at[1], prompt_sum.at[:, my_piece, :], rr_send, rr_recv.at[y], 0, head)

    @pl.when(xc == 0)
    def _():
        for slot in range(1, ROW):
            rx_copy(slot).wait_recv()
            sum_y[...] += part_x[slot].astype(jnp.float32)

        @pl.when(y > 0)
        def _():
            sum_x[1] = sum_y[...].astype(jnp.bfloat16)
            rr_copy().start()

    for j in range(heads_here):
        cols = slice(j * HD, (j + 1) * HD)
        dq[:, cols] = (dot(win_t[0], probs[1, j], NN).T * inv_scale).astype(jnp.bfloat16)
    dq_copy = pltpu.make_async_copy(dq, query_grad, store_sem.at[1])
    dq_copy.start()

    for off in range(1, REACH):
        @pl.when(leaf + off < leaves)
        def _():
            grad_copy(off).wait_recv()
            own_grad[...] += near[off].astype(jnp.float32)

    @pl.when(leaf == 0)
    def _():
        own_grad[:, :piece, :] += sum_y[...]
        for other in range(1, rows_y):
            rows = slice(other * piece, (other + 1) * piece)
            remote(
                sum_x.at[1], prompt_sum.at[:, rows, :], rr_send, rr_recv.at[other], 0, head
            ).wait_recv()
            own_grad[:, rows, :] += prompt_sum[:, rows, :].astype(jnp.float32)

    final[...] = own_grad[...].astype(jnp.bfloat16)
    last = [
        pltpu.make_async_copy(final.at[0], key_grad, store_sem.at[2]),
        pltpu.make_async_copy(final.at[1], value_grad, store_sem.at[3]),
    ]
    for copy in last:
        copy.start()

    for off in range(1, groups):
        a2a_copy(off).wait_send()
    for off in range(1, REACH):
        pl.when(leaf + off < leaves)(lambda off=off: shift_copy(off).wait_send())
        pl.when(leaf >= off)(lambda off=off: grad_copy(off).wait_send())
    for off in range(1, rows_y):
        gather_copy(off).wait_send()
        ry_copy(off).wait_send()

    @pl.when(leaf == 0)
    def _():
        @pl.loop(1, leaves)
        def _(to):
            root_copy(to).wait_send()

    @pl.when(xc > 0)
    def _():
        rx_copy(xc).wait_send()

    @pl.when((xc == 0) & (y > 0))
    def _():
        rr_copy().wait_send()

    out_copy.wait()
    dq_copy.wait()
    for copy in last:
        copy.wait()


def on_device(leaves, groups, queries, key_rows, value_rows, out_grad, ancestry, block_fill):
    tok, width = queries.shape
    heads_here = width // HD
    wide = BLK + REACH * tok
    piece = BLK // (leaves // ROW)
    bf16, f32 = jnp.bfloat16, jnp.float32
    anywhere = pl.BlockSpec(memory_space=pl.ANY)
    dma = pltpu.SemaphoreType.DMA
    return pl.pallas_call(
        functools.partial(kernel, leaves, groups),
        out_shape=(
            jax.ShapeDtypeStruct((tok, width), bf16),
            jax.ShapeDtypeStruct((tok, width), bf16),
            jax.ShapeDtypeStruct((tok, HD), bf16),
            jax.ShapeDtypeStruct((tok, HD), bf16),
        ),
        in_specs=[anywhere] * 5 + [pl.BlockSpec(memory_space=pltpu.SMEM)],
        out_specs=(anywhere,) * 4,
        scratch_shapes=[
            pltpu.VMEM((tok, width), bf16),
            pltpu.VMEM((tok, width), bf16),
            pltpu.VMEM((2,) + key_rows.shape, bf16),
            pltpu.VMEM((2, wide, HD), bf16),
            pltpu.VMEM((2, HD, wide), bf16),
            pltpu.VMEM((wide, tok), f32),
            pltpu.VMEM((heads_here, wide, tok), f32),
            pltpu.VMEM((heads_here, wide, tok), f32),
            pltpu.VMEM((heads_here, 8, tok), f32),
            pltpu.VMEM((2, heads_here, wide, tok), bf16),
            pltpu.VMEM((tok, width), bf16),
            pltpu.VMEM((tok, width), bf16),
            pltpu.VMEM((REACH, 2, tok, HD), bf16),
            pltpu.VMEM((2, tok, HD), f32),
            pltpu.VMEM((2, BLK, HD), f32),
            pltpu.VMEM((2, BLK, HD), bf16),
            pltpu.VMEM((REACH, 2, tok, HD), bf16),
            pltpu.VMEM((leaves // ROW, 2, piece, HD), bf16),
            pltpu.VMEM((2, piece, HD), f32),
            pltpu.VMEM((ROW, 2, piece, HD), bf16),
            pltpu.VMEM((2, 2, piece, HD), bf16),
            pltpu.VMEM((2, BLK, HD), bf16),
            pltpu.VMEM((2, tok, HD), bf16),
            pltpu.SMEM((8, ancestry.shape[1]), jnp.int32),
            dma((5,)),
            dma((4,)),
            dma((groups,)),
            dma((groups,)),
            dma((REACH,)),
            dma((REACH,)),
            dma((leaves,)),
            dma,
            dma((leaves // ROW,)),
            dma((leaves // ROW,)),
            dma((REACH,)),
            dma((REACH,)),
            dma((leaves // ROW,)),
            dma((leaves // ROW,)),
            dma,
            dma((ROW,)),
            dma,
            dma((leaves // ROW,)),
        ],
        compiler_params=pltpu.CompilerParams(
            collective_id=0, has_side_effects=True, vmem_limit_bytes=50 * 2**20
        ),
    )(queries, key_rows, value_rows, out_grad, ancestry, block_fill)


def solution(mesh):
    placed = (
        P("leaf", "head"),
        P(("leaf", "head"), None),
        P(("leaf", "head"), None),
        P("leaf", "head"),
        P(),
        P(),
    )
    return jax.shard_map(
        functools.partial(on_device, mesh.shape["leaf"], mesh.shape["head"]),
        mesh=mesh,
        in_specs=placed,
        out_specs=(P("leaf", "head"), P("leaf", "head"), P("leaf", "head"), P("leaf", "head")),
        check_vma=False,
    )
```

time: 461 us -> 63.4 us (0.14)
  the two profiles are of different devices: /device:TPU:1 before, /device:TPU:64 now
where the time goes in v1:
time: 63.4 us; the launch traced here: 63 us
  Pallas kernels  54.4 us (86%)
  local copies, waits for them, and re-layouts  7.91 us (12%)
  between operations  0.66 us (1%)
    pallas_call x1, Pallas kernels, on_device(): pl.pallas_call(functools.partial(kernel, leaves, groups), out_shape=(jax....  54.4 us
    unnamed x16, local copies, waits for them, and re-layouts  7.91 us

profile of v1, /device:TPU:64, one launch (start us, length us, event | category | flops | bytes accessed | tf_op | source)
XLA Modules:
  0.0 63.0 jit_solution(11255500724101702785)
XLA Ops:
  0.6 0.0 copy-start
  0.6 1.0 %copy-done = bf16[256,768]{1,0:T(8,128)(2,1)S(1)} copy-done((bf16[256,768]{1,0:T(8,128)(2,1)S(1)}, bf16[256,768]{1,0:T(8,128)(2,1)}, u32[]{:S(2)}) %copy-start) | copy-done | bytes 393240
  1.6 0.0 copy-start.1
  1.6 1.0 %copy-done.1 = bf16[256,768]{1,0:T(8,128)(2,1)S(1)} copy-done((bf16[256,768]{1,0:T(8,128)(2,1)S(1)}, bf16[256,768]{1,0:T(8,128)(2,1)}, u32[]{:S(2)}) %copy-start.1) | copy-done | bytes 393240
  2.6 0.0 copy-start.2
  2.6 0.8 %copy-done.2 = bf16[32,1024]{1,0:T(8,128)(2,1)S(1)} copy-done((bf16[32,1024]{1,0:T(8,128)(2,1)S(1)}, bf16[32,1024]{1,0:T(8,128)(2,1)}, u32[]{:S(2)}) %copy-start.2) | copy-done | bytes 65560
  3.5 0.0 copy-start.3
  3.5 0.8 %copy-done.3 = bf16[32,1024]{1,0:T(8,128)(2,1)S(1)} copy-done((bf16[32,1024]{1,0:T(8,128)(2,1)S(1)}, bf16[32,1024]{1,0:T(8,128)(2,1)}, u32[]{:S(2)}) %copy-start.3) | copy-done | bytes 65560
  4.3 0.0 copy-start.4
  4.3 0.8 %copy-done.4 = s32[128,128]{1,0:T(8,128)S(1)} copy-done((s32[128,128]{1,0:T(8,128)S(1)}, s32[128,128]{1,0:T(8,128)}, u32[]{:S(2)}) %copy-start.4) | copy-done | bytes 65560
  5.1 0.0 copy-start.5
  5.1 0.7 %copy-done.5 = s32[128]{0:T(128)S(1)} copy-done((s32[128]{0:T(128)S(1)}, s32[128]{0:T(128)}, u32[]{:S(2)}) %copy-start.5) | copy-done | bytes 536
  5.8 54.4 %shard_map.93 = (bf16[256,768]{1,0:T(8,128)(2,1)S(1)}, bf16[256,768]{1,0:T(8,128)(2,1)S(1)}, bf16[256,128]{1,0:T(8,128)(2,1)S(1)}, bf16[256,128]{1,0:T(8,128)(2,1)S(1)}) custom-call(bf16[256,768]{1,0:T(8,128)(2,1)S(1)} %copy-done, bf16[32,1024]{1,0:T(8,128)(2,1)S(1)} %copy-done.2, bf16[32,1024]{1,0:T(8,128)(2,1)S(1)} %copy-done.3, ...), custom_call_target="tpu_custom_call" | custom-call | tf_op jit(solution)/shard_map/pallas_call | solution.py:349
  60.3 0.7 %copy.14 = bf16[256,768]{1,0:T(8,128)(2,1)} copy(bf16[256,768]{1,0:T(8,128)(2,1)S(1)} %get-tuple-element.8) | data formatting | bytes 786432
  61.0 0.7 %copy.15 = bf16[256,768]{1,0:T(8,128)(2,1)} copy(bf16[256,768]{1,0:T(8,128)(2,1)S(1)} %get-tuple-element.9) | data formatting | bytes 786432
  61.8 0.6 copy.16
  62.4 0.6 copy.17
Async XLA Ops:
  0.6 1.0 %copy-start = (bf16[256,768]{1,0:T(8,128)(2,1)S(1)}, bf16[256,768]{1,0:T(8,128)(2,1)}, u32[]{:S(2)}) copy-start(bf16[256,768]{1,0:T(8,128)(2,1)} %queries.1) | copy-start | bytes 1179652
  1.6 1.0 %copy-start.1 = (bf16[256,768]{1,0:T(8,128)(2,1)S(1)}, bf16[256,768]{1,0:T(8,128)(2,1)}, u32[]{:S(2)}) copy-start(bf16[256,768]{1,0:T(8,128)(2,1)} %out_grad.1) | copy-start | bytes 1179652
  2.6 0.8 %copy-start.2 = (bf16[32,1024]{1,0:T(8,128)(2,1)S(1)}, bf16[32,1024]{1,0:T(8,128)(2,1)}, u32[]{:S(2)}) copy-start(bf16[32,1024]{1,0:T(8,128)(2,1)} %key_rows.1) | copy-start | bytes 196612
  3.5 0.8 %copy-start.3 = (bf16[32,1024]{1,0:T(8,128)(2,1)S(1)}, bf16[32,1024]{1,0:T(8,128)(2,1)}, u32[]{:S(2)}) copy-start(bf16[32,1024]{1,0:T(8,128)(2,1)} %value_rows.1) | copy-start | bytes 196612
  4.3 0.8 %copy-start.4 = (s32[128,128]{1,0:T(8,128)S(1)}, s32[128,128]{1,0:T(8,128)}, u32[]{:S(2)}) copy-start(s32[128,128]{1,0:T(8,128)} %ancestry.1) | copy-start | bytes 196612
  5.1 0.7 %copy-start.5 = (s32[128]{0:T(128)S(1)}, s32[128]{0:T(128)}, u32[]{:S(2)}) copy-start(s32[128]{0:T(128)} %block_fill.1) | copy-start | bytes 1540

commit v2 on v1

v2 whole, which is shorter than its diff:
```python
import functools
import math

import jax
import jax.numpy as jnp
from jax import lax
from jax.experimental import pallas as pl
from jax.experimental.pallas import tpu as pltpu
from jax.sharding import PartitionSpec as P

HD = 128
BLK = 128
REACH = 4
ROW = 8
MESH = pl.DeviceIdType.MESH
NEG = -1e30
NT = (((1,), (1,)), ((), ()))
NN = (((1,), (0,)), ((), ()))
dot = functools.partial(lax.dot_general, preferred_element_type=jnp.float32)


def kernel(
    leaves, groups, queries, key_rows, value_rows, out_grad, ancestry, fills,
    attn_out, query_grad, key_grad, value_grad,
    q, g, kv_in, win, win_t, bias, scores, d_weights, row_max, probs, attn, dq,
    grads, own_grad, prompt_grad, prompt_bf, near, part_x, sum_x, part_root,
    final, anc, block_fill,
    load_sem, store_sem, a2a_send, a2a_recv, shift_send, shift_recv, root_send, root_recv,
    gather_send, gather_recv, grad_send, grad_recv, rx_send, rx_recv, rr_send, rr_recv,
):
    leaf = lax.axis_index("leaf")
    head = lax.axis_index("head")
    tok = q.shape[0]
    heads_here = q.shape[1] // HD
    rows_in = kv_in.shape[1]
    rows_y = leaves // ROW
    piece = BLK // ROW
    wide = win.shape[1]
    own0 = wide - tok
    y = leaf // ROW
    xc = leaf % ROW
    core = leaf % 2
    sibling = leaf + 1 - 2 * core
    inv_scale = 1.0 / math.sqrt(HD)
    log_scale = inv_scale * math.log2(math.e)

    base = pl.multiple_of((2 * leaf) // 8 * 8, 8)
    loads = [
        pltpu.make_async_copy(key_rows, kv_in.at[0], load_sem.at[0]),
        pltpu.make_async_copy(value_rows, kv_in.at[1], load_sem.at[1]),
        pltpu.make_async_copy(queries, q, load_sem.at[2]),
        pltpu.make_async_copy(out_grad, g, load_sem.at[3]),
        pltpu.make_async_copy(ancestry.at[pl.ds(base, 8)], anc, load_sem.at[4]),
        pltpu.make_async_copy(fills, block_fill, load_sem.at[5]),
    ]
    for load in loads:
        load.start()

    pending = []
    barrier = pltpu.get_barrier_semaphore()

    def greet(leaf_to, head_to):
        pl.semaphore_signal(barrier, inc=1, device_id=(leaf_to, head_to), device_id_type=MESH)

    for off in range(1, groups):
        greet(leaf, lax.rem(head + off, groups))
    for off in range(1, ROW):
        greet(y * ROW + lax.rem(xc + off, ROW), head)
    for off in range(1, REACH):
        pl.when(leaf >= off)(functools.partial(greet, leaf - off, head))
        pl.when(leaf + off < leaves)(functools.partial(greet, leaf + off, head))

    @pl.when(leaf > 0)
    def _():
        greet(0, head)

    @pl.when(leaf == 0)
    def _():
        @pl.loop(1, leaves)
        def _(to):
            greet(to, head)

    for load in loads[:2]:
        load.wait()
    greeted = groups - 1 + ROW - 1 + jnp.minimum(leaf, REACH - 1) + jnp.minimum(leaves - 1 - leaf, REACH - 1)
    greeted += jnp.where(leaf == 0, leaves - 1, 1)
    pl.semaphore_wait(barrier, greeted)

    def remote(src, dst, send, recv, leaf_to, head_to):
        return pltpu.make_async_remote_copy(
            src_ref=src, dst_ref=dst, send_sem=send, recv_sem=recv,
            device_id=(leaf_to, head_to), device_id_type=MESH,
        )

    def a2a_copy(off):
        to = lax.rem(head + off, groups)
        return remote(
            kv_in.at[:, :, pl.ds(pl.multiple_of(to * HD, HD), HD)],
            win.at[:, pl.ds(pl.multiple_of(own0 + head * rows_in, 32), rows_in), :],
            a2a_send.at[off], a2a_recv.at[off], leaf, to,
        )

    for off in range(1, groups):
        a2a_copy(off).start()
        pending.append(a2a_copy(off).wait_send)
    win[:, pl.ds(pl.multiple_of(own0 + head * rows_in, 32), rows_in), :] = kv_in[
        :, :, pl.ds(pl.multiple_of(head * HD, HD), HD)
    ]
    for off in range(1, REACH):
        rows = pl.ds(own0 - off * tok, tok)

        @pl.when(leaf < off)
        def _():
            win[:, rows, :] = jnp.zeros((2, tok, HD), win.dtype)

    loads[4].wait()
    loads[5].wait()
    key_iota = lax.broadcasted_iota(jnp.int32, (BLK, BLK), 0)
    query_iota = lax.broadcasted_iota(jnp.int32, (BLK, BLK), 1)
    blocks_dev = tok // BLK
    for col in range(wide // BLK):
        block = 0 if col == 0 else (leaf - (REACH - 1)) * blocks_dev + col - 1
        at = 0 if col == 0 else jnp.maximum(block, 0)
        fill = block_fill[at]
        for row in range(blocks_dev):
            link = anc[2 * leaf - base + row, at]
            if col > 0:
                link = jnp.where(block >= 1, link, 0)
            limit = jnp.where(link == 1, fill, 0)
            allowed = (key_iota < limit) & (
                key_iota + block * BLK <= query_iota + (leaf * blocks_dev + row) * BLK
            )
            bias[col * BLK : (col + 1) * BLK, row * BLK : (row + 1) * BLK] = jnp.where(allowed, 0.0, NEG)
    row_max[...] = jnp.full_like(row_max, NEG)

    for off in range(1, groups):
        a2a_copy(off).wait_recv()

    def chunk(off):
        return pl.ds(pl.multiple_of(own0 - off * tok, BLK), tok)

    side = jnp.where(core == 0, 1, REACH - 1)

    def shift_copy(off):
        return remote(
            win.at[:, pl.ds(own0, tok), :], win.at[:, chunk(off), :],
            shift_send.at[off], shift_recv.at[off], leaf + off, head,
        )

    def swap_copy():
        lands = REACH - side
        return remote(
            win.at[:, chunk(2), :], win.at[:, chunk(lands), :], shift_send.at[0], shift_recv.at[lands], sibling, head
        )

    def root_copy(to):
        at = to % ROW * piece
        return remote(
            win.at[:, pl.ds(pl.multiple_of(own0 + at, piece), piece), :],
            win.at[:, pl.ds(pl.multiple_of(at, piece), piece), :],
            root_send.at[to], root_recv, to, head,
        )

    for off in (2, side):
        @pl.when(leaf + off < leaves)
        def _():
            shift_copy(off).start()

        pending.append(lambda off=off: pl.when(leaf + off < leaves)(lambda: shift_copy(off).wait_send()))

    @pl.when(leaf == 0)
    def _():
        for row in sorted(range(rows_y), key=lambda r: -min(r, rows_y - r)):
            @pl.loop(row * ROW + (row == 0), (row + 1) * ROW)
            def _(to):
                root_copy(to).start()

        win[:, :piece, :] = win[:, own0 : own0 + piece, :]

    def root_done():
        @pl.when(leaf == 0)
        def _():
            @pl.loop(1, leaves)
            def _(to):
                root_copy(to).wait_send()

    pending.append(root_done)

    loads[2].wait()
    loads[3].wait()

    def meet(first, count):
        rows = slice(first, first + count)
        keys, values, added = win[0, rows], win[1, rows], bias[rows]
        for j in range(heads_here):
            cols = slice(j * HD, (j + 1) * HD)
            part = dot(keys, q[:, cols], NT) + added
            scores[j, rows] = part
            row_max[j] = jnp.maximum(row_max[j], part.reshape(count // 8, 8, tok).max(0))
            d_weights[j, rows] = dot(values, g[:, cols], NT)

    meet(own0, tok)

    my_piece = pl.ds(pl.multiple_of(xc * piece, piece), piece)

    def gather_copy(off):
        return remote(
            win.at[:, my_piece, :], win.at[:, my_piece, :],
            gather_send.at[off], gather_recv.at[off], y * ROW + lax.rem(xc + off, ROW), head,
        )

    @pl.when(leaf >= 2)
    def _():
        shift_copy(2).wait_recv()
        swap_copy().start()

    pending.append(lambda: pl.when(leaf >= 2)(lambda: swap_copy().wait_send()))
    meet(own0 - 2 * tok, tok)

    @pl.when(leaf > 0)
    def _():
        root_copy(leaf).wait_recv()

    for off in range(1, ROW):
        gather_copy(off).start()
        pending.append(gather_copy(off).wait_send)
    for off in (1, 3):
        pl.when(leaf >= off)(lambda off=off: shift_copy(off).wait_recv())
        meet(own0 - off * tok, tok)
    for off in range(1, ROW):
        gather_copy(off).wait_recv()
    meet(0, BLK)
    win_t[0] = win[0].T
    win_t[1] = win[1].T

    step = BLK
    for j in range(heads_here):
        cols = slice(j * HD, (j + 1) * HD)
        top = jnp.max(row_max[j], axis=0, keepdims=True) * log_scale
        total = jnp.zeros((8, tok), jnp.float32)
        delta = jnp.zeros((8, tok), jnp.float32)
        for r in range(0, wide, step):
            rows = slice(r, r + step)
            e = jnp.exp2(scores[j, rows] * log_scale - top)
            scores[j, rows] = e
            total += e.reshape(step // 8, 8, tok).sum(0)
            delta += (e * d_weights[j, rows]).reshape(step // 8, 8, tok).sum(0)
        inverse = 1.0 / total.sum(0, keepdims=True)
        delta = delta.sum(0, keepdims=True) * inverse
        for r in range(0, wide, step):
            rows = slice(r, r + step)
            w = scores[j, rows] * inverse
            probs[0, j, rows] = w.astype(jnp.bfloat16)
            probs[1, j, rows] = (w * (d_weights[j, rows] - delta)).astype(jnp.bfloat16)
        attn[:, cols] = dot(win_t[1], probs[0, j], NN).T.astype(jnp.bfloat16)
    out_copy = pltpu.make_async_copy(attn, attn_out, store_sem.at[0])
    out_copy.start()
    pending.append(out_copy.wait)

    def grad_of(rows, count):
        dk = jnp.zeros((count, HD), jnp.float32)
        dv = jnp.zeros((count, HD), jnp.float32)
        for j in range(heads_here):
            cols = slice(j * HD, (j + 1) * HD)
            dk += dot(probs[1, j, rows], q[:, cols], NN)
            dv += dot(probs[0, j, rows], g[:, cols], NN)
        return dk * inv_scale, dv

    def rx_copy(off):
        to = lax.rem(xc + off, ROW)
        return remote(
            prompt_bf.at[:, pl.ds(pl.multiple_of(to * piece, piece), piece), :], part_x.at[off],
            rx_send.at[off], rx_recv.at[off], y * ROW + to, head,
        )

    dk, dv = grad_of(slice(0, BLK), BLK)
    prompt_grad[0], prompt_grad[1] = dk, dv
    prompt_bf[0], prompt_bf[1] = dk.astype(jnp.bfloat16), dv.astype(jnp.bfloat16)
    for off in range(1, ROW):
        rx_copy(off).start()
        pending.append(rx_copy(off).wait_send)

    def grad_copy(slot, to):
        return remote(grads.at[slot], near.at[slot], grad_send.at[slot], grad_recv.at[slot], to, head)

    dk, dv = grad_of(chunk(side), tok)
    grads[0, 0], grads[0, 1] = dk.astype(jnp.bfloat16), dv.astype(jnp.bfloat16)
    pl.when(leaf >= 2)(lambda: grad_copy(0, sibling).start())
    pending.append(lambda: pl.when(leaf >= 2)(lambda: grad_copy(0, sibling).wait_send()))

    own_grad[0], own_grad[1] = grad_of(chunk(2), tok)

    @pl.when(leaf >= 2)
    def _():
        grad_copy(0, sibling).wait_recv()
        grads[1] = (own_grad[...] + near[0].astype(jnp.float32)).astype(jnp.bfloat16)
        grad_copy(1, leaf - 2).start()

    pending.append(lambda: pl.when(leaf >= 2)(lambda: grad_copy(1, leaf - 2).wait_send()))

    rest = REACH - side
    dk, dv = grad_of(chunk(rest), tok)
    grads[2, 0], grads[2, 1] = dk.astype(jnp.bfloat16), dv.astype(jnp.bfloat16)
    pl.when(leaf >= rest)(lambda: grad_copy(2, leaf - rest).start())
    pending.append(lambda: pl.when(leaf >= rest)(lambda: grad_copy(2, leaf - rest).wait_send()))

    def rr_copy():
        return remote(sum_x, part_root.at[leaf], rr_send, rr_recv, 0, head)

    total_x = prompt_grad[:, my_piece, :]
    for off in range(1, ROW):
        rx_copy(off).wait_recv()
        total_x += part_x[off].astype(jnp.float32)
    sum_x[...] = total_x.astype(jnp.bfloat16)

    @pl.when(leaf > 0)
    def _():
        rr_copy().start()

    pending.append(lambda: pl.when(leaf > 0)(lambda: rr_copy().wait_send()))

    own_grad[0], own_grad[1] = grad_of(slice(own0, wide), tok)

    for j in range(heads_here):
        cols = slice(j * HD, (j + 1) * HD)
        dq[:, cols] = (dot(win_t[0], probs[1, j], NN).T * inv_scale).astype(jnp.bfloat16)
    dq_copy = pltpu.make_async_copy(dq, query_grad, store_sem.at[1])
    dq_copy.start()
    pending.append(dq_copy.wait)

    for slot, off in ((1, 2), (2, side)):
        @pl.when(leaf + off < leaves)
        def _():
            grad_copy(slot, leaf).wait_recv()
            own_grad[...] += near[slot].astype(jnp.float32)

    @pl.when(leaf == 0)
    def _():
        others = part_root.at[pl.ds(1, leaves - 1)]
        remote(others, others, rr_send, rr_recv, leaf, head).wait_recv()
        part_root[0] = sum_x[...]
        for slot in range(ROW):
            rows = slice(slot * piece, (slot + 1) * piece)
            for row in range(rows_y):
                own_grad[:, rows, :] += part_root[row * ROW + slot].astype(jnp.float32)

    final[...] = own_grad[...].astype(jnp.bfloat16)
    last = [
        pltpu.make_async_copy(final.at[0], key_grad, store_sem.at[2]),
        pltpu.make_async_copy(final.at[1], value_grad, store_sem.at[3]),
    ]
    for copy in last:
        copy.start()
        pending.append(copy.wait)

    for wait in pending:
        wait()


def store(*refs):
    held, load_sem, store_sem = refs[8:12], refs[12], refs[13]
    loads = [pltpu.make_async_copy(refs[i], held[i], load_sem.at[i]) for i in range(4)]
    stores = [pltpu.make_async_copy(held[i], refs[4 + i], store_sem.at[i]) for i in range(4)]
    for copy in loads:
        copy.start()
    for load, copy in zip(loads, stores):
        load.wait()
        copy.start()
    for copy in stores:
        copy.wait()


def on_device(leaves, groups, queries, key_rows, value_rows, out_grad, ancestry, block_fill):
    tok, width = queries.shape
    heads_here = width // HD
    wide = BLK + REACH * tok
    piece = BLK // ROW
    bf16, f32 = jnp.bfloat16, jnp.float32
    anywhere = pl.BlockSpec(memory_space=pl.ANY)
    in_hbm = pl.BlockSpec(memory_space=pltpu.HBM)
    dma = pltpu.SemaphoreType.DMA
    held = pl.pallas_call(
        functools.partial(kernel, leaves, groups),
        out_shape=(
            jax.ShapeDtypeStruct((tok, width), bf16),
            jax.ShapeDtypeStruct((tok, width), bf16),
            jax.ShapeDtypeStruct((tok, HD), bf16),
            jax.ShapeDtypeStruct((tok, HD), bf16),
        ),
        in_specs=[in_hbm] * 6,
        out_specs=(anywhere,) * 4,
        scratch_shapes=[
            pltpu.VMEM((tok, width), bf16),
            pltpu.VMEM((tok, width), bf16),
            pltpu.VMEM((2,) + key_rows.shape, bf16),
            pltpu.VMEM((2, wide, HD), bf16),
            pltpu.VMEM((2, HD, wide), bf16),
            pltpu.VMEM((wide, tok), f32),
            pltpu.VMEM((heads_here, wide, tok), f32),
            pltpu.VMEM((heads_here, wide, tok), f32),
            pltpu.VMEM((heads_here, 8, tok), f32),
            pltpu.VMEM((2, heads_here, wide, tok), bf16),
            pltpu.VMEM((tok, width), bf16),
            pltpu.VMEM((tok, width), bf16),
            pltpu.VMEM((REACH, 2, tok, HD), bf16),
            pltpu.VMEM((2, tok, HD), f32),
            pltpu.VMEM((2, BLK, HD), f32),
            pltpu.VMEM((2, BLK, HD), bf16),
            pltpu.VMEM((REACH, 2, tok, HD), bf16),
            pltpu.VMEM((ROW, 2, piece, HD), bf16),
            pltpu.VMEM((2, piece, HD), bf16),
            pltpu.VMEM((leaves, 2, piece, HD), bf16),
            pltpu.VMEM((2, tok, HD), bf16),
            pltpu.SMEM((8, ancestry.shape[1]), jnp.int32),
            pltpu.SMEM(block_fill.shape, jnp.int32),
            dma((6,)),
            dma((4,)),
            dma((groups,)),
            dma((groups,)),
            dma((REACH,)),
            dma((REACH,)),
            dma((leaves,)),
            dma,
            dma((ROW,)),
            dma((ROW,)),
            dma((REACH,)),
            dma((REACH,)),
            dma((ROW,)),
            dma((ROW,)),
            dma,
            dma,
        ],
        compiler_params=pltpu.CompilerParams(
            collective_id=0, has_side_effects=True, vmem_limit_bytes=58 * 2**20
        ),
    )(queries, key_rows, value_rows, out_grad, ancestry, block_fill)
    return pl.pallas_call(
        store,
        out_shape=[jax.ShapeDtypeStruct(a.shape, a.dtype) for a in held],
        in_specs=[anywhere] * 4,
        out_specs=[in_hbm] * 4,
        scratch_shapes=[pltpu.VMEM(a.shape, a.dtype) for a in held] + [dma((4,)), dma((4,))],
        compiler_params=pltpu.CompilerParams(vmem_limit_bytes=58 * 2**20),
    )(*held)


def solution(mesh):
    placed = (
        P("leaf", "head"),
        P(("leaf", "head"), None),
        P(("leaf", "head"), None),
        P("leaf", "head"),
        P(),
        P(),
    )
    return jax.shard_map(
        functools.partial(on_device, mesh.shape["leaf"], mesh.shape["head"]),
        mesh=mesh,
        in_specs=placed,
        out_specs=(P("leaf", "head"), P("leaf", "head"), P("leaf", "head"), P("leaf", "head")),
        check_vma=False,
    )
```

time: 63.4 us -> 48 us (0.76)
  the two profiles are of different devices: /device:TPU:64 before, /device:TPU:5 now
where the time goes in v2:
time: 48 us; the launch traced here: 47.9 us
  Pallas kernels  47.2 us (98%)
  between operations  0.64 us (1%)
    pallas_call x1, Pallas kernels, on_device(): pl.pallas_call(functools.partial(kernel, leaves, groups), out_shape=(jax....  45.3 us
    pallas_call x1, Pallas kernels, on_device(): pl.pallas_call(store, out_shape=[jax.ShapeDtypeStruct(a.shape, a.dtype) f...  1.98 us

profile of v2, /device:TPU:5, one launch (start us, length us, event | category | flops | bytes accessed | tf_op | source)
XLA Modules:
  0.0 47.9 jit_solution(6826331722534072047)
XLA Ops:
  0.6 45.3 %shard_map.93 = (bf16[256,768]{1,0:T(8,128)(2,1)}, bf16[256,768]{1,0:T(8,128)(2,1)}, bf16[256,128]{1,0:T(8,128)(2,1)}, bf16[256,128]{1,0:T(8,128)(2,1)}) custom-call(bf16[256,768]{1,0:T(8,128)(2,1)} %queries.1, bf16[32,1024]{1,0:T(8,128)(2,1)} %key_rows.1, bf16[32,1024]{1,0:T(8,128)(2,1)} %value_rows.1, bf16[256,768]{1,0:T(8,128)(2,1)} %out_grad.1, ...), custom_call_target="tpu_custom_call" | custom-call | tf_op jit(solution)/shard_map/pallas_call | solution.py:382
  45.9 2.0 %shard_map.94 = (bf16[256,768]{1,0:T(8,128)(2,1)}, bf16[256,768]{1,0:T(8,128)(2,1)}, bf16[256,128]{1,0:T(8,128)(2,1)}, bf16[256,128]{1,0:T(8,128)(2,1)}) custom-call(bf16[256,768]{1,0:T(8,128)(2,1)} %get-tuple-element.8.refs_0_, bf16[256,768]{1,0:T(8,128)(2,1)} %get-tuple-element.9.refs_1_, bf16[256,128]{1,0:T(8,128)(2,1)} %get-tuple-element.10.refs_2_, ...), custom_call_target="tpu_custom_call" | custom-call | tf_op jit(solution)/shard_map/pallas_call | solution.py:437

commit v3 on v2

--- a/solution.py
+++ b/solution.py
@@ -22,7 +22,7 @@
 def kernel(
     leaves, groups, queries, key_rows, value_rows, out_grad, ancestry, fills,
     attn_out, query_grad, key_grad, value_grad,
-    q, g, kv_in, win, win_t, bias, scores, d_weights, row_max, probs, attn, dq,
+    q, g, kv_in, win, win_t, bias, scores, d_weights, stats, probs, attn, dq,
     grads, own_grad, prompt_grad, prompt_bf, near, part_x, sum_x, part_root,
     final, anc, block_fill,
     load_sem, store_sem, a2a_send, a2a_recv, shift_send, shift_recv, root_send, root_recv,
@@ -131,26 +131,26 @@
                 key_iota + block * BLK <= query_iota + (leaf * blocks_dev + row) * BLK
             )
             bias[col * BLK : (col + 1) * BLK, row * BLK : (row + 1) * BLK] = jnp.where(allowed, 0.0, NEG)
-    row_max[...] = jnp.full_like(row_max, NEG)
-
-    for off in range(1, groups):
-        a2a_copy(off).wait_recv()
-
-    def chunk(off):
-        return pl.ds(pl.multiple_of(own0 - off * tok, BLK), tok)
 
     side = jnp.where(core == 0, 1, REACH - 1)
 
-    def shift_copy(off):
-        return remote(
-            win.at[:, pl.ds(own0, tok), :], win.at[:, chunk(off), :],
-            shift_send.at[off], shift_recv.at[off], leaf + off, head,
-        )
-
-    def swap_copy():
+    parts = max(1, groups // 2)
+    part_rows = tok // parts
+
+    def part_of(off, part):
+        return win.at[:, pl.ds(pl.multiple_of(own0 - off * tok + part * part_rows, 32), part_rows), :]
+
+    def shift_copy(off, part):
+        return remote(
+            part_of(0, part), part_of(off, part),
+            shift_send.at[off, part], shift_recv.at[off, part], leaf + off, head,
+        )
+
+    def swap_copy(part):
         lands = REACH - side
         return remote(
-            win.at[:, chunk(2), :], win.at[:, chunk(lands), :], shift_send.at[0], shift_recv.at[lands], sibling, head
+            part_of(2, part), part_of(lands, part),
+            shift_send.at[0, part], shift_recv.at[lands, part], sibling, head,
         )
 
     def root_copy(to):
@@ -161,21 +161,30 @@
             root_send.at[to], root_recv, to, head,
         )
 
-    for off in (2, side):
-        @pl.when(leaf + off < leaves)
-        def _():
-            shift_copy(off).start()
-
-        pending.append(lambda off=off: pl.when(leaf + off < leaves)(lambda: shift_copy(off).wait_send()))
-
-    @pl.when(leaf == 0)
-    def _():
+    def scatter():
         for row in sorted(range(rows_y), key=lambda r: -min(r, rows_y - r)):
             @pl.loop(row * ROW + (row == 0), (row + 1) * ROW)
             def _(to):
                 root_copy(to).start()
 
         win[:, :piece, :] = win[:, own0 : own0 + piece, :]
+
+    per_part = groups // parts
+    for part in range(parts):
+        for source in range(part * per_part, (part + 1) * per_part):
+            off = lax.rem(head - source + groups, groups)
+            pl.when(off > 0)(lambda off=off: a2a_copy(off).wait_recv())
+        if part * part_rows < BLK <= (part + 1) * part_rows:
+            pl.when(leaf == 0)(scatter)
+        for off in (2, side):
+            pl.when(leaf + off < leaves)(lambda off=off: shift_copy(off, part).start())
+
+    def shift_done():
+        for part in range(parts):
+            for off in (2, side):
+                pl.when(leaf + off < leaves)(lambda off=off: shift_copy(off, part).wait_send())
+
+    pending.append(shift_done)
 
     def root_done():
         @pl.when(leaf == 0)
@@ -189,17 +198,28 @@
     loads[2].wait()
     loads[3].wait()
 
-    def meet(first, count):
+    def meet(slot, first, count):
         rows = slice(first, first + count)
         keys, values, added = win[0, rows], win[1, rows], bias[rows]
         for j in range(heads_here):
             cols = slice(j * HD, (j + 1) * HD)
             part = dot(keys, q[:, cols], NT) + added
             scores[j, rows] = part
-            row_max[j] = jnp.maximum(row_max[j], part.reshape(count // 8, 8, tok).max(0))
+            top = part.reshape(count // 8, 8, tok).max(0).max(0, keepdims=True) * log_scale
             d_weights[j, rows] = dot(values, g[:, cols], NT)
-
-    meet(own0, tok)
+            total = jnp.zeros((8, tok), jnp.float32)
+            delta = jnp.zeros((8, tok), jnp.float32)
+            for r in range(first, first + count, BLK):
+                some = slice(r, r + BLK)
+                e = jnp.exp2(scores[j, some] * log_scale - top)
+                scores[j, some] = e
+                total += e.reshape(BLK // 8, 8, tok).sum(0)
+                delta += (e * d_weights[j, some]).reshape(BLK // 8, 8, tok).sum(0)
+            stats[slot, j, 0:1] = top
+            stats[slot, j, 1:2] = total.sum(0, keepdims=True)
+            stats[slot, j, 2:3] = delta.sum(0, keepdims=True)
+
+    meet(1, own0, tok)
 
     my_piece = pl.ds(pl.multiple_of(xc * piece, piece), piece)
 
@@ -208,14 +228,6 @@
             win.at[:, my_piece, :], win.at[:, my_piece, :],
             gather_send.at[off], gather_recv.at[off], y * ROW + lax.rem(xc + off, ROW), head,
         )
-
-    @pl.when(leaf >= 2)
-    def _():
-        shift_copy(2).wait_recv()
-        swap_copy().start()
-
-    pending.append(lambda: pl.when(leaf >= 2)(lambda: swap_copy().wait_send()))
-    meet(own0 - 2 * tok, tok)
 
     @pl.when(leaf > 0)
     def _():
@@ -224,40 +236,49 @@
     for off in range(1, ROW):
         gather_copy(off).start()
         pending.append(gather_copy(off).wait_send)
+
+    @pl.when(leaf >= 2)
+    def _():
+        for part in range(parts):
+            shift_copy(2, part).wait_recv()
+            swap_copy(part).start()
+
+    def swap_done():
+        for part in range(parts):
+            swap_copy(part).wait_send()
+
+    pending.append(lambda: pl.when(leaf >= 2)(swap_done))
+    meet(3, own0 - 2 * tok, tok)
+
     for off in (1, 3):
-        pl.when(leaf >= off)(lambda off=off: shift_copy(off).wait_recv())
-        meet(own0 - off * tok, tok)
+        @pl.when(leaf >= off)
+        def _():
+            for part in range(parts):
+                shift_copy(off, part).wait_recv()
+
+        meet(off + 1, own0 - off * tok, tok)
     for off in range(1, ROW):
         gather_copy(off).wait_recv()
-    meet(0, BLK)
-    win_t[0] = win[0].T
-    win_t[1] = win[1].T
-
-    step = BLK
+    meet(0, 0, BLK)
+
     for j in range(heads_here):
-        cols = slice(j * HD, (j + 1) * HD)
-        top = jnp.max(row_max[j], axis=0, keepdims=True) * log_scale
-        total = jnp.zeros((8, tok), jnp.float32)
-        delta = jnp.zeros((8, tok), jnp.float32)
-        for r in range(0, wide, step):
-            rows = slice(r, r + step)
-            e = jnp.exp2(scores[j, rows] * log_scale - top)
-            scores[j, rows] = e
-            total += e.reshape(step // 8, 8, tok).sum(0)
-            delta += (e * d_weights[j, rows]).reshape(step // 8, 8, tok).sum(0)
-        inverse = 1.0 / total.sum(0, keepdims=True)
-        delta = delta.sum(0, keepdims=True) * inverse
-        for r in range(0, wide, step):
-            rows = slice(r, r + step)
-            w = scores[j, rows] * inverse
-            probs[0, j, rows] = w.astype(jnp.bfloat16)
-            probs[1, j, rows] = (w * (d_weights[j, rows] - delta)).astype(jnp.bfloat16)
-        attn[:, cols] = dot(win_t[1], probs[0, j], NN).T.astype(jnp.bfloat16)
-    out_copy = pltpu.make_async_copy(attn, attn_out, store_sem.at[0])
-    out_copy.start()
-    pending.append(out_copy.wait)
-
-    def grad_of(rows, count):
+        tops = [stats[slot, j, 0:1] for slot in range(REACH + 1)]
+        top = functools.reduce(jnp.maximum, tops)
+        scales = [jnp.exp2(t - top) for t in tops]
+        inverse = 1.0 / sum(stats[slot, j, 1:2] * scales[slot] for slot in range(REACH + 1))
+        stats[0, j, 4:5] = inverse * sum(stats[slot, j, 2:3] * scales[slot] for slot in range(REACH + 1))
+        for slot in range(REACH + 1):
+            stats[slot, j, 3:4] = inverse * scales[slot]
+
+    def grad_of(slot, first, count):
+        for j in range(heads_here):
+            factor, delta = stats[slot, j, 3:4], stats[0, j, 4:5]
+            for r in range(0, count, BLK):
+                some = pl.ds(pl.multiple_of(first + r, BLK), BLK)
+                w = scores[j, some] * factor
+                probs[0, j, some] = w.astype(jnp.bfloat16)
+                probs[1, j, some] = (w * (d_weights[j, some] - delta)).astype(jnp.bfloat16)
+        rows = pl.ds(pl.multiple_of(first, BLK), count)
         dk = jnp.zeros((count, HD), jnp.float32)
         dv = jnp.zeros((count, HD), jnp.float32)
         for j in range(heads_here):
@@ -273,7 +294,7 @@
             rx_send.at[off], rx_recv.at[off], y * ROW + to, head,
         )
 
-    dk, dv = grad_of(slice(0, BLK), BLK)
+    dk, dv = grad_of(0, 0, BLK)
     prompt_grad[0], prompt_grad[1] = dk, dv
     prompt_bf[0], prompt_bf[1] = dk.astype(jnp.bfloat16), dv.astype(jnp.bfloat16)
     for off in range(1, ROW):
@@ -283,12 +304,12 @@
     def grad_copy(slot, to):
         return remote(grads.at[slot], near.at[slot], grad_send.at[slot], grad_recv.at[slot], to, head)
 
-    dk, dv = grad_of(chunk(side), tok)
+    dk, dv = grad_of(side + 1, own0 - side * tok, tok)
     grads[0, 0], grads[0, 1] = dk.astype(jnp.bfloat16), dv.astype(jnp.bfloat16)
     pl.when(leaf >= 2)(lambda: grad_copy(0, sibling).start())
     pending.append(lambda: pl.when(leaf >= 2)(lambda: grad_copy(0, sibling).wait_send()))
 
-    own_grad[0], own_grad[1] = grad_of(chunk(2), tok)
+    own_grad[0], own_grad[1] = grad_of(3, own0 - 2 * tok, tok)
 
     @pl.when(leaf >= 2)
     def _():
@@ -299,7 +320,7 @@
     pending.append(lambda: pl.when(leaf >= 2)(lambda: grad_copy(1, leaf - 2).wait_send()))
 
     rest = REACH - side
-    dk, dv = grad_of(chunk(rest), tok)
+    dk, dv = grad_of(rest + 1, own0 - rest * tok, tok)
     grads[2, 0], grads[2, 1] = dk.astype(jnp.bfloat16), dv.astype(jnp.bfloat16)
     pl.when(leaf >= rest)(lambda: grad_copy(2, leaf - rest).start())
     pending.append(lambda: pl.when(leaf >= rest)(lambda: grad_copy(2, leaf - rest).wait_send()))
@@ -319,8 +340,16 @@
 
     pending.append(lambda: pl.when(leaf > 0)(lambda: rr_copy().wait_send()))
 
-    own_grad[0], own_grad[1] = grad_of(slice(own0, wide), tok)
-
+    own_grad[0], own_grad[1] = grad_of(1, own0, tok)
+
+    win_t[0] = win[0].T
+    win_t[1] = win[1].T
+    for j in range(heads_here):
+        cols = slice(j * HD, (j + 1) * HD)
+        attn[:, cols] = dot(win_t[1], probs[0, j], NN).T.astype(jnp.bfloat16)
+    out_copy = pltpu.make_async_copy(attn, attn_out, store_sem.at[0])
+    out_copy.start()
+    pending.append(out_copy.wait)
     for j in range(heads_here):
         cols = slice(j * HD, (j + 1) * HD)
         dq[:, cols] = (dot(win_t[0], probs[1, j], NN).T * inv_scale).astype(jnp.bfloat16)
@@ -358,15 +387,10 @@
 
 
 def store(*refs):
-    held, load_sem, store_sem = refs[8:12], refs[12], refs[13]
-    loads = [pltpu.make_async_copy(refs[i], held[i], load_sem.at[i]) for i in range(4)]
-    stores = [pltpu.make_async_copy(held[i], refs[4 + i], store_sem.at[i]) for i in range(4)]
-    for copy in loads:
+    copies = [pltpu.make_async_copy(refs[i], refs[4 + i], refs[8].at[i]) for i in range(4)]
+    for copy in copies:
         copy.start()
-    for load, copy in zip(loads, stores):
-        load.wait()
-        copy.start()
-    for copy in stores:
+    for copy in copies:
         copy.wait()
 
 
@@ -382,10 +406,10 @@
     held = pl.pallas_call(
         functools.partial(kernel, leaves, groups),
         out_shape=(
-            jax.ShapeDtypeStruct((tok, width), bf16),
-            jax.ShapeDtypeStruct((tok, width), bf16),
-            jax.ShapeDtypeStruct((tok, HD), bf16),
-            jax.ShapeDtypeStruct((tok, HD), bf16),
+            pltpu.VMEM((tok, width), bf16),
+            pltpu.VMEM((tok, width), bf16),
+            pltpu.VMEM((tok, HD), bf16),
+            pltpu.VMEM((tok, HD), bf16),
         ),
         in_specs=[in_hbm] * 6,
         out_specs=(anywhere,) * 4,
@@ -398,7 +422,7 @@
             pltpu.VMEM((wide, tok), f32),
             pltpu.VMEM((heads_here, wide, tok), f32),
             pltpu.VMEM((heads_here, wide, tok), f32),
-            pltpu.VMEM((heads_here, 8, tok), f32),
+            pltpu.VMEM((REACH + 1, heads_here, 8, tok), f32),
             pltpu.VMEM((2, heads_here, wide, tok), bf16),
             pltpu.VMEM((tok, width), bf16),
             pltpu.VMEM((tok, width), bf16),
@@ -417,8 +441,8 @@
             dma((4,)),
             dma((groups,)),
             dma((groups,)),
-            dma((REACH,)),
-            dma((REACH,)),
+            dma((REACH, max(1, groups // 2))),
+            dma((REACH, max(1, groups // 2))),
             dma((leaves,)),
             dma,
             dma((ROW,)),
@@ -431,17 +455,21 @@
             dma,
         ],
         compiler_params=pltpu.CompilerParams(
-            collective_id=0, has_side_effects=True, vmem_limit_bytes=58 * 2**20
+            collective_id=0, has_side_effects=True, vmem_limit_bytes=50 * 2**20
         ),
-    )(queries, key_rows, value_rows, out_grad, ancestry, block_fill)
+    )(
+        *(
+            pltpu.with_memory_space_constraint(a, pltpu.HBM)
+            for a in (queries, key_rows, value_rows, out_grad, ancestry, block_fill)
+        )
+    )
     return pl.pallas_call(
         store,
         out_shape=[jax.ShapeDtypeStruct(a.shape, a.dtype) for a in held],
         in_specs=[anywhere] * 4,
         out_specs=[in_hbm] * 4,
-        scratch_shapes=[pltpu.VMEM(a.shape, a.dtype) for a in held] + [dma((4,)), dma((4,))],
-        compiler_params=pltpu.CompilerParams(vmem_limit_bytes=58 * 2**20),
-    )(*held)
+        scratch_shapes=[dma((4,))],
+    )(*(pltpu.with_memory_space_constraint(a, pltpu.VMEM) for a in held))
 
 
 def solution(mesh):

time: 48 us -> 41.5 us (0.86)
  the two profiles are of different devices: /device:TPU:5 before, /device:TPU:1 now
where the time goes in v3:
time: 41.5 us; the launch traced here: 41.3 us
  Pallas kernels  40.7 us (98%)
  between operations  0.64 us (2%)
    pallas_call x1, Pallas kernels, on_device(): pl.pallas_call(functools.partial(kernel, leaves, groups), out_shape=(pltp...  39.8 us
    pallas_call x1, Pallas kernels, on_device(): pl.pallas_call(store, out_shape=[jax.ShapeDtypeStruct(a.shape, a.dtype) f...  0.95 us

profile of v3, /device:TPU:1, one launch (start us, length us, event | category | flops | bytes accessed | tf_op | source)
XLA Modules:
  0.0 41.3 jit_solution(10784503018278063976)
XLA Ops:
  0.6 39.8 %shard_map.93 = (bf16[256,768]{1,0:T(8,128)(2,1)S(1)}, bf16[256,768]{1,0:T(8,128)(2,1)S(1)}, bf16[256,128]{1,0:T(8,128)(2,1)S(1)}, bf16[256,128]{1,0:T(8,128)(2,1)S(1)}) custom-call(bf16[256,768]{1,0:T(8,128)(2,1)} %queries.1, bf16[32,1024]{1,0:T(8,128)(2,1)} %key_rows.1, bf16[32,1024]{1,0:T(8,128)(2,1)} %value_rows.1, bf16[256,768]{1,0:T(8,128)(2,1)} %out_grad.1, ...), custom_call_target="tpu_custom_call" | custom-call | tf_op jit(solution)/shard_map/pallas_call | solution.py:406
  40.4 0.9 %shard_map.94 = (bf16[256,768]{1,0:T(8,128)(2,1)}, bf16[256,768]{1,0:T(8,128)(2,1)}, bf16[256,128]{1,0:T(8,128)(2,1)}, bf16[256,128]{1,0:T(8,128)(2,1)}) custom-call(bf16[256,768]{1,0:T(8,128)(2,1)S(1)} %get-tuple-element.8.refs_0_, bf16[256,768]{1,0:T(8,128)(2,1)S(1)} %get-tuple-element.9.refs_1_, bf16[256,128]{1,0:T(8,128)(2,1)S(1)} %get-tuple-element.10.refs_2_, ...), custom_call_target="tpu_custom_call" | custom-call | tf_op jit(solution)/shard_map/pallas_call | solution.py:466

commit v4 on v3

--- a/solution.py
+++ b/solution.py
@@ -26,7 +26,7 @@
     grads, own_grad, prompt_grad, prompt_bf, near, part_x, sum_x, part_root,
     final, anc, block_fill,
     load_sem, store_sem, a2a_send, a2a_recv, shift_send, shift_recv, root_send, root_recv,
-    gather_send, gather_recv, grad_send, grad_recv, rx_send, rx_recv, rr_send, rr_recv,
+    gather_send, gather_recv, grad_send, grad_recv, rx_send, rx_recv, rr_send, rr_recv, ready,
 ):
     leaf = lax.axis_index("leaf")
     head = lax.axis_index("head")
@@ -34,11 +34,13 @@
     heads_here = q.shape[1] // HD
     rows_in = kv_in.shape[1]
     rows_y = leaves // ROW
-    piece = BLK // ROW
+    chips = ROW // 2
+    piece = BLK // chips
     wide = win.shape[1]
     own0 = wide - tok
     y = leaf // ROW
     xc = leaf % ROW
+    x = xc // 2
     core = leaf % 2
     sibling = leaf + 1 - 2 * core
     inv_scale = 1.0 / math.sqrt(HD)
@@ -53,7 +55,7 @@
         pltpu.make_async_copy(ancestry.at[pl.ds(base, 8)], anc, load_sem.at[4]),
         pltpu.make_async_copy(fills, block_fill, load_sem.at[5]),
     ]
-    for load in loads:
+    for load in loads[:2]:
         load.start()
 
     pending = []
@@ -70,10 +72,6 @@
         pl.when(leaf >= off)(functools.partial(greet, leaf - off, head))
         pl.when(leaf + off < leaves)(functools.partial(greet, leaf + off, head))
 
-    @pl.when(leaf > 0)
-    def _():
-        greet(0, head)
-
     @pl.when(leaf == 0)
     def _():
         @pl.loop(1, leaves)
@@ -83,8 +81,12 @@
     for load in loads[:2]:
         load.wait()
     greeted = groups - 1 + ROW - 1 + jnp.minimum(leaf, REACH - 1) + jnp.minimum(leaves - 1 - leaf, REACH - 1)
-    greeted += jnp.where(leaf == 0, leaves - 1, 1)
+    greeted += jnp.where(leaf == 0, 0, 1)
     pl.semaphore_wait(barrier, greeted)
+
+    @pl.when((leaf > 0) & (core == 0))
+    def _():
+        pl.semaphore_signal(ready, inc=1, device_id=(0, head), device_id_type=MESH)
 
     def remote(src, dst, send, recv, leaf_to, head_to):
         return pltpu.make_async_remote_copy(
@@ -103,6 +105,8 @@
     for off in range(1, groups):
         a2a_copy(off).start()
         pending.append(a2a_copy(off).wait_send)
+    for load in loads[2:]:
+        load.start()
     win[:, pl.ds(pl.multiple_of(own0 + head * rows_in, 32), rows_in), :] = kv_in[
         :, :, pl.ds(pl.multiple_of(head * HD, HD), HD)
     ]
@@ -154,7 +158,7 @@
         )
 
     def root_copy(to):
-        at = to % ROW * piece
+        at = to % ROW // 2 * piece
         return remote(
             win.at[:, pl.ds(pl.multiple_of(own0 + at, piece), piece), :],
             win.at[:, pl.ds(pl.multiple_of(at, piece), piece), :],
@@ -162,10 +166,11 @@
         )
 
     def scatter():
+        pl.semaphore_wait(ready, rows_y * chips - 1)
         for row in sorted(range(rows_y), key=lambda r: -min(r, rows_y - r)):
-            @pl.loop(row * ROW + (row == 0), (row + 1) * ROW)
-            def _(to):
-                root_copy(to).start()
+            @pl.loop(int(row == 0), chips)
+            def _(i):
+                root_copy(row * ROW + 2 * i).start()
 
         win[:, :piece, :] = win[:, own0 : own0 + piece, :]
 
@@ -174,10 +179,10 @@
         for source in range(part * per_part, (part + 1) * per_part):
             off = lax.rem(head - source + groups, groups)
             pl.when(off > 0)(lambda off=off: a2a_copy(off).wait_recv())
+        for off in (2, side):
+            pl.when(leaf + off < leaves)(lambda off=off: shift_copy(off, part).start())
         if part * part_rows < BLK <= (part + 1) * part_rows:
             pl.when(leaf == 0)(scatter)
-        for off in (2, side):
-            pl.when(leaf + off < leaves)(lambda off=off: shift_copy(off, part).start())
 
     def shift_done():
         for part in range(parts):
@@ -189,9 +194,9 @@
     def root_done():
         @pl.when(leaf == 0)
         def _():
-            @pl.loop(1, leaves)
-            def _(to):
-                root_copy(to).wait_send()
+            @pl.loop(1, rows_y * chips)
+            def _(i):
+                root_copy(2 * i).wait_send()
 
     pending.append(root_done)
 
@@ -221,21 +226,29 @@
 
     meet(1, own0, tok)
 
-    my_piece = pl.ds(pl.multiple_of(xc * piece, piece), piece)
+    my_piece = pl.ds(pl.multiple_of(x * piece, piece), piece)
 
     def gather_copy(off):
         return remote(
             win.at[:, my_piece, :], win.at[:, my_piece, :],
-            gather_send.at[off], gather_recv.at[off], y * ROW + lax.rem(xc + off, ROW), head,
-        )
-
-    @pl.when(leaf > 0)
-    def _():
-        root_copy(leaf).wait_recv()
-
-    for off in range(1, ROW):
-        gather_copy(off).start()
-        pending.append(gather_copy(off).wait_send)
+            gather_send.at[off], gather_recv.at[x], y * ROW + lax.rem(xc + off, ROW), head,
+        )
+
+    def gather_got(slot):
+        rows = win.at[:, slot * piece : (slot + 1) * piece, :]
+        return remote(rows, rows, gather_send.at[0], gather_recv.at[slot], leaf, head)
+
+    @pl.when(core == 0)
+    def _():
+        pl.when(leaf > 0)(lambda: root_copy(leaf).wait_recv())
+        for off in range(1, ROW):
+            gather_copy(off).start()
+
+    def gather_done():
+        for off in range(1, ROW):
+            gather_copy(off).wait_send()
+
+    pending.append(lambda: pl.when(core == 0)(gather_done))
 
     @pl.when(leaf >= 2)
     def _():
@@ -257,8 +270,8 @@
                 shift_copy(off, part).wait_recv()
 
         meet(off + 1, own0 - off * tok, tok)
-    for off in range(1, ROW):
-        gather_copy(off).wait_recv()
+    for slot in range(chips):
+        pl.when((core == 1) | (x != slot))(lambda slot=slot: gather_got(slot).wait_recv())
     meet(0, 0, BLK)
 
     for j in range(heads_here):
@@ -287,19 +300,21 @@
             dv += dot(probs[0, j, rows], g[:, cols], NN)
         return dk * inv_scale, dv
 
-    def rx_copy(off):
-        to = lax.rem(xc + off, ROW)
+    def rx_copy(slot):
         return remote(
-            prompt_bf.at[:, pl.ds(pl.multiple_of(to * piece, piece), piece), :], part_x.at[off],
-            rx_send.at[off], rx_recv.at[off], y * ROW + to, head,
-        )
+            prompt_bf.at[:, slot * piece : (slot + 1) * piece, :], part_x.at[xc],
+            rx_send.at[slot], rx_recv.at[xc], y * ROW + 2 * slot, head,
+        )
+
+    def rx_got(slot):
+        return remote(part_x.at[slot], part_x.at[slot], rx_send.at[0], rx_recv.at[slot], leaf, head)
 
     dk, dv = grad_of(0, 0, BLK)
     prompt_grad[0], prompt_grad[1] = dk, dv
     prompt_bf[0], prompt_bf[1] = dk.astype(jnp.bfloat16), dv.astype(jnp.bfloat16)
-    for off in range(1, ROW):
-        rx_copy(off).start()
-        pending.append(rx_copy(off).wait_send)
+    for slot in range(chips):
+        pl.when(xc != 2 * slot)(lambda slot=slot: rx_copy(slot).start())
+        pending.append(lambda slot=slot: pl.when(xc != 2 * slot)(lambda: rx_copy(slot).wait_send()))
 
     def grad_copy(slot, to):
         return remote(grads.at[slot], near.at[slot], grad_send.at[slot], grad_recv.at[slot], to, head)
@@ -308,16 +323,6 @@
     grads[0, 0], grads[0, 1] = dk.astype(jnp.bfloat16), dv.astype(jnp.bfloat16)
     pl.when(leaf >= 2)(lambda: grad_copy(0, sibling).start())
     pending.append(lambda: pl.when(leaf >= 2)(lambda: grad_copy(0, sibling).wait_send()))
-
-    own_grad[0], own_grad[1] = grad_of(3, own0 - 2 * tok, tok)
-
-    @pl.when(leaf >= 2)
-    def _():
-        grad_copy(0, sibling).wait_recv()
-        grads[1] = (own_grad[...] + near[0].astype(jnp.float32)).astype(jnp.bfloat16)
-        grad_copy(1, leaf - 2).start()
-
-    pending.append(lambda: pl.when(leaf >= 2)(lambda: grad_copy(1, leaf - 2).wait_send()))
 
     rest = REACH - side
     dk, dv = grad_of(rest + 1, own0 - rest * tok, tok)
@@ -325,20 +330,30 @@
     pl.when(leaf >= rest)(lambda: grad_copy(2, leaf - rest).start())
     pending.append(lambda: pl.when(leaf >= rest)(lambda: grad_copy(2, leaf - rest).wait_send()))
 
+    own_grad[0], own_grad[1] = grad_of(3, own0 - 2 * tok, tok)
+
+    @pl.when(leaf >= 2)
+    def _():
+        grad_copy(0, sibling).wait_recv()
+        grads[1] = (own_grad[...] + near[0].astype(jnp.float32)).astype(jnp.bfloat16)
+        grad_copy(1, leaf - 2).start()
+
+    pending.append(lambda: pl.when(leaf >= 2)(lambda: grad_copy(1, leaf - 2).wait_send()))
+
     def rr_copy():
-        return remote(sum_x, part_root.at[leaf], rr_send, rr_recv, 0, head)
-
-    total_x = prompt_grad[:, my_piece, :]
-    for off in range(1, ROW):
-        rx_copy(off).wait_recv()
-        total_x += part_x[off].astype(jnp.float32)
-    sum_x[...] = total_x.astype(jnp.bfloat16)
-
-    @pl.when(leaf > 0)
-    def _():
-        rr_copy().start()
-
-    pending.append(lambda: pl.when(leaf > 0)(lambda: rr_copy().wait_send()))
+        return remote(sum_x, part_root.at[leaf // 2], rr_send, rr_recv, 0, head)
+
+    @pl.when(core == 0)
+    def _():
+        sum_all = prompt_grad[:, my_piece, :]
+        for off in range(1, ROW):
+            slot = lax.rem(xc + off, ROW)
+            rx_got(slot).wait_recv()
+            sum_all += part_x[slot].astype(jnp.float32)
+        sum_x[...] = sum_all.astype(jnp.bfloat16)
+        pl.when(leaf > 0)(lambda: rr_copy().start())
+
+    pending.append(lambda: pl.when((core == 0) & (leaf > 0))(lambda: rr_copy().wait_send()))
 
     own_grad[0], own_grad[1] = grad_of(1, own0, tok)
 
@@ -365,13 +380,13 @@
 
     @pl.when(leaf == 0)
     def _():
-        others = part_root.at[pl.ds(1, leaves - 1)]
+        others = part_root.at[pl.ds(1, rows_y * chips - 1)]
         remote(others, others, rr_send, rr_recv, leaf, head).wait_recv()
         part_root[0] = sum_x[...]
-        for slot in range(ROW):
+        for slot in range(chips):
             rows = slice(slot * piece, (slot + 1) * piece)
             for row in range(rows_y):
-                own_grad[:, rows, :] += part_root[row * ROW + slot].astype(jnp.float32)
+                own_grad[:, rows, :] += part_root[row * chips + slot].astype(jnp.float32)
 
     final[...] = own_grad[...].astype(jnp.bfloat16)
     last = [
@@ -398,7 +413,8 @@
     tok, width = queries.shape
     heads_here = width // HD
     wide = BLK + REACH * tok
-    piece = BLK // ROW
+    chips = ROW // 2
+    piece = BLK // chips
     bf16, f32 = jnp.bfloat16, jnp.float32
     anywhere = pl.BlockSpec(memory_space=pl.ANY)
     in_hbm = pl.BlockSpec(memory_space=pltpu.HBM)
@@ -433,7 +449,7 @@
             pltpu.VMEM((REACH, 2, tok, HD), bf16),
             pltpu.VMEM((ROW, 2, piece, HD), bf16),
             pltpu.VMEM((2, piece, HD), bf16),
-            pltpu.VMEM((leaves, 2, piece, HD), bf16),
+            pltpu.VMEM((leaves // 2, 2, piece, HD), bf16),
             pltpu.VMEM((2, tok, HD), bf16),
             pltpu.SMEM((8, ancestry.shape[1]), jnp.int32),
             pltpu.SMEM(block_fill.shape, jnp.int32),
@@ -453,6 +469,7 @@
             dma((ROW,)),
             dma,
             dma,
+            pltpu.SemaphoreType.REGULAR,
         ],
         compiler_params=pltpu.CompilerParams(
             collective_id=0, has_side_effects=True, vmem_limit_bytes=50 * 2**20

time: 41.5 us -> 41.7 us (level)
  the two profiles are of different devices: /device:TPU:1 before, /device:TPU:64 now
where the time goes in v4:
time: 41.7 us; the launch traced here: 41.5 us
  Pallas kernels  40.9 us (98%)
  between operations  0.64 us (2%)
    pallas_call x1, Pallas kernels, on_device(): pl.pallas_call(functools.partial(kernel, leaves, groups), out_shape=(pltp...  39.9 us
    pallas_call x1, Pallas kernels, on_device(): pl.pallas_call(store, out_shape=[jax.ShapeDtypeStruct(a.shape, a.dtype) f...  0.95 us

profile of v4, /device:TPU:64, one launch (start us, length us, event | category | flops | bytes accessed | tf_op | source)
XLA Modules:
  0.0 41.5 jit_solution(7734063413890903551)
XLA Ops:
  0.6 39.9 %shard_map.93 = (bf16[256,768]{1,0:T(8,128)(2,1)S(1)}, bf16[256,768]{1,0:T(8,128)(2,1)S(1)}, bf16[256,128]{1,0:T(8,128)(2,1)S(1)}, bf16[256,128]{1,0:T(8,128)(2,1)S(1)}) custom-call(bf16[256,768]{1,0:T(8,128)(2,1)} %queries.1, bf16[32,1024]{1,0:T(8,128)(2,1)} %key_rows.1, bf16[32,1024]{1,0:T(8,128)(2,1)} %value_rows.1, bf16[256,768]{1,0:T(8,128)(2,1)} %out_grad.1, ...), custom_call_target="tpu_custom_call" | custom-call | tf_op jit(solution)/shard_map/pallas_call | solution.py:422
  40.6 0.9 %shard_map.94 = (bf16[256,768]{1,0:T(8,128)(2,1)}, bf16[256,768]{1,0:T(8,128)(2,1)}, bf16[256,128]{1,0:T(8,128)(2,1)}, bf16[256,128]{1,0:T(8,128)(2,1)}) custom-call(bf16[256,768]{1,0:T(8,128)(2,1)S(1)} %get-tuple-element.8.refs_0_, bf16[256,768]{1,0:T(8,128)(2,1)S(1)} %get-tuple-element.9.refs_1_, bf16[256,128]{1,0:T(8,128)(2,1)S(1)} %get-tuple-element.10.refs_2_, ...), custom_call_target="tpu_custom_call" | custom-call | tf_op jit(solution)/shard_map/pallas_call | solution.py:483

commit v5 on v4

--- a/solution.py
+++ b/solution.py
@@ -26,7 +26,7 @@
     grads, own_grad, prompt_grad, prompt_bf, near, part_x, sum_x, part_root,
     final, anc, block_fill,
     load_sem, store_sem, a2a_send, a2a_recv, shift_send, shift_recv, root_send, root_recv,
-    gather_send, gather_recv, grad_send, grad_recv, rx_send, rx_recv, rr_send, rr_recv, ready,
+    gather_send, gather_recv, grad_send, grad_recv, rx_send, rx_recv, rr_send, rr_recv, ready, zready,
 ):
     leaf = lax.axis_index("leaf")
     head = lax.axis_index("head")
@@ -43,6 +43,8 @@
     x = xc // 2
     core = leaf % 2
     sibling = leaf + 1 - 2 * core
+    half = groups // 2
+    lower = head < half
     inv_scale = 1.0 / math.sqrt(HD)
     log_scale = inv_scale * math.log2(math.e)
 
@@ -65,7 +67,8 @@
         pl.semaphore_signal(barrier, inc=1, device_id=(leaf_to, head_to), device_id_type=MESH)
 
     for off in range(1, groups):
-        greet(leaf, lax.rem(head + off, groups))
+        to = lax.rem(head + off, groups)
+        pl.when(lower | (to >= half))(functools.partial(greet, leaf, to))
     for off in range(1, ROW):
         greet(y * ROW + lax.rem(xc + off, ROW), head)
     for off in range(1, REACH):
@@ -80,13 +83,18 @@
 
     for load in loads[:2]:
         load.wait()
-    greeted = groups - 1 + ROW - 1 + jnp.minimum(leaf, REACH - 1) + jnp.minimum(leaves - 1 - leaf, REACH - 1)
+    greeted = jnp.where(lower, half, groups) - 1 + ROW - 1 + jnp.minimum(leaf, REACH - 1) + jnp.minimum(leaves - 1 - leaf, REACH - 1)
     greeted += jnp.where(leaf == 0, 0, 1)
     pl.semaphore_wait(barrier, greeted)
 
     @pl.when((leaf > 0) & (core == 0))
     def _():
         pl.semaphore_signal(ready, inc=1, device_id=(0, head), device_id_type=MESH)
+
+    @pl.when(head >= half)
+    def _():
+        for to in range(half):
+            pl.semaphore_signal(zready, inc=1, device_id=(leaf, to), device_id_type=MESH)
 
     def remote(src, dst, send, recv, leaf_to, head_to):
         return pltpu.make_async_remote_copy(
@@ -103,7 +111,8 @@
         )
 
     for off in range(1, groups):
-        a2a_copy(off).start()
+        to = lax.rem(head + off, groups)
+        pl.when((head >= half) | (to < half))(lambda off=off: a2a_copy(off).start())
         pending.append(a2a_copy(off).wait_send)
     for load in loads[2:]:
         load.start()
@@ -174,6 +183,11 @@
 
         win[:, :piece, :] = win[:, own0 : own0 + piece, :]
 
+    def send_upper():
+        pl.semaphore_wait(zready, groups - half)
+        for to in range(half, groups):
+            a2a_copy(to - head).start()
+
     per_part = groups // parts
     for part in range(parts):
         for source in range(part * per_part, (part + 1) * per_part):
@@ -183,6 +197,7 @@
             pl.when(leaf + off < leaves)(lambda off=off: shift_copy(off, part).start())
         if part * part_rows < BLK <= (part + 1) * part_rows:
             pl.when(leaf == 0)(scatter)
+            pl.when(lower)(send_upper)
 
     def shift_done():
         for part in range(parts):
@@ -470,6 +485,7 @@
             dma,
             dma,
             pltpu.SemaphoreType.REGULAR,
+            pltpu.SemaphoreType.REGULAR,
         ],
         compiler_params=pltpu.CompilerParams(
             collective_id=0, has_side_effects=True, vmem_limit_bytes=50 * 2**20

time: 41.7 us -> 39.9 us (0.957)
  Pallas kernels: 40.9 us -> 39.1 us
    pallas_call x1, Pallas kernels: 39.9 us -> 38.2 us  [on_device(): pl.pallas_call(functools.partial(kernel, leaves, groups), out_shape=(pltp...]
where the time goes in v5:
time: 39.9 us; the launch traced here: 39.7 us
  Pallas kernels  39.1 us (98%)
  between operations  0.64 us (2%)
    pallas_call x1, Pallas kernels, on_device(): pl.pallas_call(functools.partial(kernel, leaves, groups), out_shape=(pltp...  38.2 us
    pallas_call x1, Pallas kernels, on_device(): pl.pallas_call(store, out_shape=[jax.ShapeDtypeStruct(a.shape, a.dtype) f...  0.95 us

profile of v5, /device:TPU:64, one launch (start us, length us, event | category | flops | bytes accessed | tf_op | source)
XLA Modules:
  0.0 39.7 jit_solution(4620584011613802922)
XLA Ops:
  0.6 38.2 %shard_map.93 = (bf16[256,768]{1,0:T(8,128)(2,1)S(1)}, bf16[256,768]{1,0:T(8,128)(2,1)S(1)}, bf16[256,128]{1,0:T(8,128)(2,1)S(1)}, bf16[256,128]{1,0:T(8,128)(2,1)S(1)}) custom-call(bf16[256,768]{1,0:T(8,128)(2,1)} %queries.1, bf16[32,1024]{1,0:T(8,128)(2,1)} %key_rows.1, bf16[32,1024]{1,0:T(8,128)(2,1)} %value_rows.1, bf16[256,768]{1,0:T(8,128)(2,1)} %out_grad.1, ...), custom_call_target="tpu_custom_call" | custom-call | tf_op jit(solution)/shard_map/pallas_call | solution.py:437
  38.8 0.9 %shard_map.94 = (bf16[256,768]{1,0:T(8,128)(2,1)}, bf16[256,768]{1,0:T(8,128)(2,1)}, bf16[256,128]{1,0:T(8,128)(2,1)}, bf16[256,128]{1,0:T(8,128)(2,1)}) custom-call(bf16[256,768]{1,0:T(8,128)(2,1)S(1)} %get-tuple-element.8.refs_0_, bf16[256,768]{1,0:T(8,128)(2,1)S(1)} %get-tuple-element.9.refs_1_, bf16[256,128]{1,0:T(8,128)(2,1)S(1)} %get-tuple-element.10.refs_2_, ...), custom_call_target="tpu_custom_call" | custom-call | tf_op jit(solution)/shard_map/pallas_call | solution.py:499

commit v6 on v5

--- a/solution.py
+++ b/solution.py
@@ -12,6 +12,7 @@
 BLK = 128
 REACH = 4
 ROW = 8
+HOLDERS = (0, 1, 2, 6)
 MESH = pl.DeviceIdType.MESH
 NEG = -1e30
 NT = (((1,), (1,)), ((), ()))
@@ -24,7 +25,7 @@
     attn_out, query_grad, key_grad, value_grad,
     q, g, kv_in, win, win_t, bias, scores, d_weights, stats, probs, attn, dq,
     grads, own_grad, prompt_grad, prompt_bf, near, part_x, sum_x, part_root,
-    final, anc, block_fill,
+    anc, block_fill,
     load_sem, store_sem, a2a_send, a2a_recv, shift_send, shift_recv, root_send, root_recv,
     gather_send, gather_recv, grad_send, grad_recv, rx_send, rx_recv, rr_send, rr_recv, ready, zready,
 ):
@@ -315,10 +316,14 @@
             dv += dot(probs[0, j, rows], g[:, cols], NN)
         return dk * inv_scale, dv
 
+    holder = (xc < 3) | (xc == 6)
+    held_slot = jnp.where(xc == 6, 3, xc)
+    held_rows = pl.ds(pl.multiple_of(held_slot * piece, piece), piece)
+
     def rx_copy(slot):
         return remote(
             prompt_bf.at[:, slot * piece : (slot + 1) * piece, :], part_x.at[xc],
-            rx_send.at[slot], rx_recv.at[xc], y * ROW + 2 * slot, head,
+            rx_send.at[slot], rx_recv.at[xc], y * ROW + HOLDERS[slot], head,
         )
 
     def rx_got(slot):
@@ -328,8 +333,8 @@
     prompt_grad[0], prompt_grad[1] = dk, dv
     prompt_bf[0], prompt_bf[1] = dk.astype(jnp.bfloat16), dv.astype(jnp.bfloat16)
     for slot in range(chips):
-        pl.when(xc != 2 * slot)(lambda slot=slot: rx_copy(slot).start())
-        pending.append(lambda slot=slot: pl.when(xc != 2 * slot)(lambda: rx_copy(slot).wait_send()))
+        pl.when(xc != HOLDERS[slot])(lambda slot=slot: rx_copy(slot).start())
+        pending.append(lambda slot=slot: pl.when(xc != HOLDERS[slot])(lambda: rx_copy(slot).wait_send()))
 
     def grad_copy(slot, to):
         return remote(grads.at[slot], near.at[slot], grad_send.at[slot], grad_recv.at[slot], to, head)
@@ -356,11 +361,11 @@
     pending.append(lambda: pl.when(leaf >= 2)(lambda: grad_copy(1, leaf - 2).wait_send()))
 
     def rr_copy():
-        return remote(sum_x, part_root.at[leaf // 2], rr_send, rr_recv, 0, head)
-
-    @pl.when(core == 0)
-    def _():
-        sum_all = prompt_grad[:, my_piece, :]
+        return remote(sum_x, part_root.at[y * chips + held_slot], rr_send, rr_recv, 0, head)
+
+    @pl.when(holder)
+    def _():
+        sum_all = prompt_grad[:, held_rows, :]
         for off in range(1, ROW):
             slot = lax.rem(xc + off, ROW)
             rx_got(slot).wait_recv()
@@ -368,7 +373,7 @@
         sum_x[...] = sum_all.astype(jnp.bfloat16)
         pl.when(leaf > 0)(lambda: rr_copy().start())
 
-    pending.append(lambda: pl.when((core == 0) & (leaf > 0))(lambda: rr_copy().wait_send()))
+    pending.append(lambda: pl.when(holder & (leaf > 0))(lambda: rr_copy().wait_send()))
 
     own_grad[0], own_grad[1] = grad_of(1, own0, tok)
 
@@ -387,6 +392,9 @@
     dq_copy.start()
     pending.append(dq_copy.wait)
 
+    for wait in pending:
+        wait()
+
     for slot, off in ((1, 2), (2, side)):
         @pl.when(leaf + off < leaves)
         def _():
@@ -400,20 +408,13 @@
         part_root[0] = sum_x[...]
         for slot in range(chips):
             rows = slice(slot * piece, (slot + 1) * piece)
+            total = own_grad[:, rows, :]
             for row in range(rows_y):
-                own_grad[:, rows, :] += part_root[row * chips + slot].astype(jnp.float32)
-
-    final[...] = own_grad[...].astype(jnp.bfloat16)
-    last = [
-        pltpu.make_async_copy(final.at[0], key_grad, store_sem.at[2]),
-        pltpu.make_async_copy(final.at[1], value_grad, store_sem.at[3]),
-    ]
-    for copy in last:
-        copy.start()
-        pending.append(copy.wait)
-
-    for wait in pending:
-        wait()
+                total += part_root[row * chips + slot].astype(jnp.float32)
+            own_grad[:, rows, :] = total
+
+    key_grad[...] = own_grad[0].astype(jnp.bfloat16)
+    value_grad[...] = own_grad[1].astype(jnp.bfloat16)
 
 
 def store(*refs):
@@ -433,6 +434,7 @@
     bf16, f32 = jnp.bfloat16, jnp.float32
     anywhere = pl.BlockSpec(memory_space=pl.ANY)
     in_hbm = pl.BlockSpec(memory_space=pltpu.HBM)
+    in_vmem = pl.BlockSpec(memory_space=pltpu.VMEM)
     dma = pltpu.SemaphoreType.DMA
     held = pl.pallas_call(
         functools.partial(kernel, leaves, groups),
@@ -443,7 +445,7 @@
             pltpu.VMEM((tok, HD), bf16),
         ),
         in_specs=[in_hbm] * 6,
-        out_specs=(anywhere,) * 4,
+        out_specs=(anywhere, anywhere, in_vmem, in_vmem),
         scratch_shapes=[
             pltpu.VMEM((tok, width), bf16),
             pltpu.VMEM((tok, width), bf16),
@@ -465,11 +467,10 @@
             pltpu.VMEM((ROW, 2, piece, HD), bf16),
             pltpu.VMEM((2, piece, HD), bf16),
             pltpu.VMEM((leaves // 2, 2, piece, HD), bf16),
-            pltpu.VMEM((2, tok, HD), bf16),
             pltpu.SMEM((8, ancestry.shape[1]), jnp.int32),
             pltpu.SMEM(block_fill.shape, jnp.int32),
             dma((6,)),
-            dma((4,)),
+            dma((2,)),
             dma((groups,)),
             dma((groups,)),
             dma((REACH, max(1, groups // 2))),

time: 39.9 us -> 39 us (0.977)
  Pallas kernels: 39.1 us -> 38.2 us
    pallas_call x1, Pallas kernels: 38.2 us -> 37.2 us  [on_device(): pl.pallas_call(functools.partial(kernel, leaves, groups), out_shape=(pltp...]
where the time goes in v6:
time: 39 us; the launch traced here: 38.8 us
  Pallas kernels  38.2 us (98%)
  between operations  0.64 us (2%)
    pallas_call x1, Pallas kernels, on_device(): pl.pallas_call(functools.partial(kernel, leaves, groups), out_shape=(pltp...  37.2 us
    pallas_call x1, Pallas kernels, on_device(): pl.pallas_call(store, out_shape=[jax.ShapeDtypeStruct(a.shape, a.dtype) f...  0.95 us

profile of v6, /device:TPU:64, one launch (start us, length us, event | category | flops | bytes accessed | tf_op | source)
XLA Modules:
  0.0 38.8 jit_solution(15444380888421833779)
XLA Ops:
  0.6 37.2 %shard_map.93 = (bf16[256,768]{1,0:T(8,128)(2,1)S(1)}, bf16[256,768]{1,0:T(8,128)(2,1)S(1)}, bf16[256,128]{1,0:T(8,128)(2,1)S(1)}, bf16[256,128]{1,0:T(8,128)(2,1)S(1)}) custom-call(bf16[256,768]{1,0:T(8,128)(2,1)} %queries.1, bf16[32,1024]{1,0:T(8,128)(2,1)} %key_rows.1, bf16[32,1024]{1,0:T(8,128)(2,1)} %value_rows.1, bf16[256,768]{1,0:T(8,128)(2,1)} %out_grad.1, ...), custom_call_target="tpu_custom_call" | custom-call | tf_op jit(solution)/shard_map/pallas_call | solution.py:439
  37.8 0.9 %shard_map.94 = (bf16[256,768]{1,0:T(8,128)(2,1)}, bf16[256,768]{1,0:T(8,128)(2,1)}, bf16[256,128]{1,0:T(8,128)(2,1)}, bf16[256,128]{1,0:T(8,128)(2,1)}) custom-call(bf16[256,768]{1,0:T(8,128)(2,1)S(1)} %get-tuple-element.8.refs_0_, bf16[256,768]{1,0:T(8,128)(2,1)S(1)} %get-tuple-element.9.refs_1_, bf16[256,128]{1,0:T(8,128)(2,1)S(1)} %get-tuple-element.10.refs_2_, ...), custom_call_target="tpu_custom_call" | custom-call | tf_op jit(solution)/shard_map/pallas_call | solution.py:500

commit v7 on v6

--- a/solution.py
+++ b/solution.py
@@ -219,28 +219,23 @@
     loads[2].wait()
     loads[3].wait()
 
-    def meet(slot, first, count):
-        rows = slice(first, first + count)
+    def meet(first):
+        slot, rows = first // BLK, slice(first, first + BLK)
         keys, values, added = win[0, rows], win[1, rows], bias[rows]
         for j in range(heads_here):
             cols = slice(j * HD, (j + 1) * HD)
             part = dot(keys, q[:, cols], NT) + added
-            scores[j, rows] = part
-            top = part.reshape(count // 8, 8, tok).max(0).max(0, keepdims=True) * log_scale
-            d_weights[j, rows] = dot(values, g[:, cols], NT)
-            total = jnp.zeros((8, tok), jnp.float32)
-            delta = jnp.zeros((8, tok), jnp.float32)
-            for r in range(first, first + count, BLK):
-                some = slice(r, r + BLK)
-                e = jnp.exp2(scores[j, some] * log_scale - top)
-                scores[j, some] = e
-                total += e.reshape(BLK // 8, 8, tok).sum(0)
-                delta += (e * d_weights[j, some]).reshape(BLK // 8, 8, tok).sum(0)
+            top = part.reshape(BLK // 8, 8, tok).max(0).max(0, keepdims=True) * log_scale
+            d = dot(values, g[:, cols], NT)
+            d_weights[j, rows] = d
+            e = jnp.exp2(part * log_scale - top)
+            scores[j, rows] = e
             stats[slot, j, 0:1] = top
-            stats[slot, j, 1:2] = total.sum(0, keepdims=True)
-            stats[slot, j, 2:3] = delta.sum(0, keepdims=True)
-
-    meet(1, own0, tok)
+            stats[slot, j, 1:2] = e.reshape(BLK // 8, 8, tok).sum(0).sum(0, keepdims=True)
+            stats[slot, j, 2:3] = (e * d).reshape(BLK // 8, 8, tok).sum(0).sum(0, keepdims=True)
+
+    for first in range(own0, wide, BLK):
+        meet(first)
 
     my_piece = pl.ds(pl.multiple_of(x * piece, piece), piece)
 
@@ -266,43 +261,51 @@
 
     pending.append(lambda: pl.when(core == 0)(gather_done))
 
-    @pl.when(leaf >= 2)
-    def _():
-        for part in range(parts):
+    early, late = range(max(1, parts // 2)), range(max(1, parts // 2), parts)
+
+    def swap(some):
+        for part in some:
             shift_copy(2, part).wait_recv()
             swap_copy(part).start()
+
+    def arrive(off, some):
+        for part in some:
+            shift_copy(off, part).wait_recv()
 
     def swap_done():
         for part in range(parts):
             swap_copy(part).wait_send()
 
     pending.append(lambda: pl.when(leaf >= 2)(swap_done))
-    meet(3, own0 - 2 * tok, tok)
-
+    pl.when(leaf >= 2)(functools.partial(swap, early))
+    meet(own0 - 2 * tok)
+    pl.when(leaf >= 2)(functools.partial(swap, late))
     for off in (1, 3):
-        @pl.when(leaf >= off)
-        def _():
-            for part in range(parts):
-                shift_copy(off, part).wait_recv()
-
-        meet(off + 1, own0 - off * tok, tok)
+        pl.when(leaf >= off)(functools.partial(arrive, off, early))
+        meet(own0 - off * tok)
+    meet(own0 - 2 * tok + BLK)
+    for off in (1, 3):
+        pl.when(leaf >= off)(functools.partial(arrive, off, late))
+        meet(own0 - off * tok + BLK)
     for slot in range(chips):
         pl.when((core == 1) | (x != slot))(lambda slot=slot: gather_got(slot).wait_recv())
-    meet(0, 0, BLK)
-
+    meet(0)
+
+    slots = wide // BLK
     for j in range(heads_here):
-        tops = [stats[slot, j, 0:1] for slot in range(REACH + 1)]
+        tops = [stats[slot, j, 0:1] for slot in range(slots)]
         top = functools.reduce(jnp.maximum, tops)
         scales = [jnp.exp2(t - top) for t in tops]
-        inverse = 1.0 / sum(stats[slot, j, 1:2] * scales[slot] for slot in range(REACH + 1))
-        stats[0, j, 4:5] = inverse * sum(stats[slot, j, 2:3] * scales[slot] for slot in range(REACH + 1))
-        for slot in range(REACH + 1):
+        inverse = 1.0 / sum(stats[slot, j, 1:2] * scales[slot] for slot in range(slots))
+        stats[0, j, 4:5] = inverse * sum(stats[slot, j, 2:3] * scales[slot] for slot in range(slots))
+        for slot in range(slots):
             stats[slot, j, 3:4] = inverse * scales[slot]
 
-    def grad_of(slot, first, count):
+    def grad_of(first, count):
         for j in range(heads_here):
-            factor, delta = stats[slot, j, 3:4], stats[0, j, 4:5]
+            delta = stats[0, j, 4:5]
             for r in range(0, count, BLK):
+                factor = stats[(first + r) // BLK, j, 3:4]
                 some = pl.ds(pl.multiple_of(first + r, BLK), BLK)
                 w = scores[j, some] * factor
                 probs[0, j, some] = w.astype(jnp.bfloat16)
@@ -329,7 +332,7 @@
     def rx_got(slot):
         return remote(part_x.at[slot], part_x.at[slot], rx_send.at[0], rx_recv.at[slot], leaf, head)
 
-    dk, dv = grad_of(0, 0, BLK)
+    dk, dv = grad_of(0, BLK)
     prompt_grad[0], prompt_grad[1] = dk, dv
     prompt_bf[0], prompt_bf[1] = dk.astype(jnp.bfloat16), dv.astype(jnp.bfloat16)
     for slot in range(chips):
@@ -339,18 +342,18 @@
     def grad_copy(slot, to):
         return remote(grads.at[slot], near.at[slot], grad_send.at[slot], grad_recv.at[slot], to, head)
 
-    dk, dv = grad_of(side + 1, own0 - side * tok, tok)
+    dk, dv = grad_of(own0 - side * tok, tok)
     grads[0, 0], grads[0, 1] = dk.astype(jnp.bfloat16), dv.astype(jnp.bfloat16)
     pl.when(leaf >= 2)(lambda: grad_copy(0, sibling).start())
     pending.append(lambda: pl.when(leaf >= 2)(lambda: grad_copy(0, sibling).wait_send()))
 
     rest = REACH - side
-    dk, dv = grad_of(rest + 1, own0 - rest * tok, tok)
+    dk, dv = grad_of(own0 - rest * tok, tok)
     grads[2, 0], grads[2, 1] = dk.astype(jnp.bfloat16), dv.astype(jnp.bfloat16)
     pl.when(leaf >= rest)(lambda: grad_copy(2, leaf - rest).start())
     pending.append(lambda: pl.when(leaf >= rest)(lambda: grad_copy(2, leaf - rest).wait_send()))
 
-    own_grad[0], own_grad[1] = grad_of(3, own0 - 2 * tok, tok)
+    own_grad[0], own_grad[1] = grad_of(own0 - 2 * tok, tok)
 
     @pl.when(leaf >= 2)
     def _():
@@ -375,7 +378,7 @@
 
     pending.append(lambda: pl.when(holder & (leaf > 0))(lambda: rr_copy().wait_send()))
 
-    own_grad[0], own_grad[1] = grad_of(1, own0, tok)
+    own_grad[0], own_grad[1] = grad_of(own0, tok)
 
     win_t[0] = win[0].T
     win_t[1] = win[1].T
@@ -455,7 +458,7 @@
             pltpu.VMEM((wide, tok), f32),
             pltpu.VMEM((heads_here, wide, tok), f32),
             pltpu.VMEM((heads_here, wide, tok), f32),
-            pltpu.VMEM((REACH + 1, heads_here, 8, tok), f32),
+            pltpu.VMEM((wide // BLK, heads_here, 8, tok), f32),
             pltpu.VMEM((2, heads_here, wide, tok), bf16),
             pltpu.VMEM((tok, width), bf16),
             pltpu.VMEM((tok, width), bf16),

time: 39 us -> 38.7 us (level)
  no operation moved by 1% of the time
where the time goes in v7:
time: 38.7 us; the launch traced here: 38.5 us
  Pallas kernels  37.9 us (98%)
  between operations  0.64 us (2%)
    pallas_call x1, Pallas kernels, on_device(): pl.pallas_call(functools.partial(kernel, leaves, groups), out_shape=(pltp...  36.9 us
    pallas_call x1, Pallas kernels, on_device(): pl.pallas_call(store, out_shape=[jax.ShapeDtypeStruct(a.shape, a.dtype) f...  0.95 us

profile of v7, /device:TPU:64, one launch (start us, length us, event | category | flops | bytes accessed | tf_op | source)
XLA Modules:
  0.0 38.5 jit_solution(9119115461086547035)
XLA Ops:
  0.6 36.9 %shard_map.93 = (bf16[256,768]{1,0:T(8,128)(2,1)S(1)}, bf16[256,768]{1,0:T(8,128)(2,1)S(1)}, bf16[256,128]{1,0:T(8,128)(2,1)S(1)}, bf16[256,128]{1,0:T(8,128)(2,1)S(1)}) custom-call(bf16[256,768]{1,0:T(8,128)(2,1)} %queries.1, bf16[32,1024]{1,0:T(8,128)(2,1)} %key_rows.1, bf16[32,1024]{1,0:T(8,128)(2,1)} %value_rows.1, bf16[256,768]{1,0:T(8,128)(2,1)} %out_grad.1, ...), custom_call_target="tpu_custom_call" | custom-call | tf_op jit(solution)/shard_map/pallas_call | solution.py:442
  37.6 0.9 %shard_map.94 = (bf16[256,768]{1,0:T(8,128)(2,1)}, bf16[256,768]{1,0:T(8,128)(2,1)}, bf16[256,128]{1,0:T(8,128)(2,1)}, bf16[256,128]{1,0:T(8,128)(2,1)}) custom-call(bf16[256,768]{1,0:T(8,128)(2,1)S(1)} %get-tuple-element.8.refs_0_, bf16[256,768]{1,0:T(8,128)(2,1)S(1)} %get-tuple-element.9.refs_1_, bf16[256,128]{1,0:T(8,128)(2,1)S(1)} %get-tuple-element.10.refs_2_, ...), custom_call_target="tpu_custom_call" | custom-call | tf_op jit(solution)/shard_map/pallas_call | solution.py:503
